TPU v7x, 32 devices: a whole 2x2x4 slice. The times are simulated.
32 devices in a mesh: dp: 8 (over y, x, core), tensor: 4 (over z).
Axes of the slice: x: 2, y: 2, z: 4, core: 2. Of those that a mesh axis runs over, the one named last changes fastest.
Arguments:
- tokens: bfloat16 [2048, 8192], P('dp'), may hold values from -64 to 64
- grad_out: bfloat16 [2048, 4096], P('dp', 'tensor'), may hold values from -0.75 to 0.75
- lengths: int32 [8], P('dp'), may hold values from 128 to 256, as said below
- weights: bfloat16 [4, 8, 256, 6144], P('tensor', None, None, 'dp'), may hold values from -0.0625 to 0.0625
- moment1: float32 [4, 8, 256, 6144], P('tensor', None, None, 'dp'), may hold values from -3 to 3
- moment2: float32 [4, 8, 256, 6144], P('tensor', None, None, 'dp'), may hold values from 0.01 to 4
Outputs:
- input_grad: bfloat16 [2048, 8192], P('dp', 'tensor')
- new_weights: bfloat16 [4, 8, 256, 6144], P(None, 'dp', None, 'tensor')
- new_first: float32 [4, 8, 256, 6144], P(None, 'dp', None, 'tensor')
- new_second: float32 [4, 8, 256, 6144], P(None, 'dp', None, 'tensor')
Inputs may be any that keep to these rules, and one draw needn't show every extreme that they name: `lengths`: each replica's length is at least half its slots; some replica fills all 256 slots.
All inputs are finite; a program needn't handle non-finite values.
Results may differ from a plain program's by a relative error of at most 0.04.
Values may be sent and summed in bfloat16 or wider, within the bound.
No kernel may reach another device: no remote copies, remote signals or barrier semaphores. Data moves between devices by JAX's collectives and lax.ppermute only.
A program may use at most 192 MiB of HBM per device.

v0:
```python
import jax
import jax.numpy as jnp
from jax import lax
from jax.sharding import PartitionSpec as P

QUERY_HEADS = 32
KEY_VALUE_HEADS = 8
HEAD_SIZE = 128


beta_first = 0.9
beta_second = 0.95
adam_eps = 1e-08
learn_rate = 0.002
decay_rate = 0.1
bias_first = 1.0 - beta_first**20
bias_second = 1.0 - beta_second**20


def adam_update(param, gradient, first, second):
    first_new = beta_first * first + (1.0 - beta_first) * gradient
    second_new = beta_second * second + (1.0 - beta_second) * gradient * gradient
    ratio = first_new / bias_first / (jnp.sqrt(second_new / bias_second) + adam_eps)
    widened = param.astype(jnp.float32)
    updated = (widened - learn_rate * (ratio + decay_rate * widened)).astype(jnp.bfloat16)
    return (updated, first_new, second_new)


def local(tokens, grad_out, lengths, weights, moment1, moment2):
    tensor_count = lax.axis_size("tensor")
    replica_count = lax.axis_size("dp")
    sequence_length, width = tokens.shape
    row_block = weights.shape[2]
    relaid = lax.all_to_all(
        lax.all_to_all(weights, "dp", split_axis=1, concat_axis=3, tiled=True),
        "tensor",
        split_axis=3,
        concat_axis=0,
        tiled=True,
    )
    block_cols = relaid.shape[3]
    query_columns = grad_out.shape[1]
    key_value_columns = (block_cols - query_columns) // 2
    kv_heads = key_value_columns // HEAD_SIZE
    query_group = QUERY_HEADS // KEY_VALUE_HEADS
    moved_first, moved_second = (
        lax.all_to_all(
            lax.all_to_all(moment1, "dp", split_axis=1, concat_axis=3, tiled=True),
            "tensor",
            split_axis=3,
            concat_axis=0,
            tiled=True,
        ),
        lax.all_to_all(
            lax.all_to_all(moment2, "dp", split_axis=1, concat_axis=3, tiled=True),
            "tensor",
            split_axis=3,
            concat_axis=0,
            tiled=True,
        ),
    )
    inputs_four = tokens.reshape(sequence_length, tensor_count, replica_count, row_block)
    gathered = lax.all_gather(relaid, "dp", axis=1, tiled=True).reshape(width, block_cols)
    projected = jnp.dot(tokens, gathered, preferred_element_type=jnp.float32)
    scale = HEAD_SIZE ** (-0.5)
    query_four = (
        projected[:, :query_columns]
        .astype(jnp.bfloat16)
        .reshape(sequence_length, kv_heads, query_group, HEAD_SIZE)
    )
    key_projected = (
        projected[:, query_columns : query_columns + key_value_columns]
        .astype(jnp.bfloat16)
        .reshape(sequence_length, kv_heads, HEAD_SIZE)
    )
    value_projected = (
        projected[:, query_columns + key_value_columns :]
        .astype(jnp.bfloat16)
        .reshape(sequence_length, kv_heads, HEAD_SIZE)
    )
    length = lengths[0]
    posit = jnp.arange(sequence_length)
    allowed = (posit[None, :] <= posit[:, None]) & (posit[None, :] < length)
    active_mask = (posit < length).astype(jnp.bfloat16)
    upstream_gradient = (
        grad_out.reshape(sequence_length, kv_heads, query_group, HEAD_SIZE)
        * active_mask[:, None, None, None]
    )
    scores = (
        jnp.einsum("sgnd,tgd->gnst", query_four, key_projected, preferred_element_type=jnp.float32)
        * scale
    )
    scores = jnp.where(allowed, scores, -jnp.inf)
    expo = jnp.exp(scores - jnp.max(scores, -1, keepdims=True))
    probs = expo / jnp.sum(expo, -1, keepdims=True)
    probs_low = probs.astype(jnp.bfloat16)
    attended = jnp.einsum(
        "gnst,tgd->sgnd", probs_low, value_projected, preferred_element_type=jnp.float32
    )
    value_gradient = jnp.einsum(
        "xoil,ixoy->lxy", probs_low, upstream_gradient, preferred_element_type=jnp.float32
    )
    dprobs = jnp.einsum(
        "sgnd,tgd->gnst", upstream_gradient, value_projected, preferred_element_type=jnp.float32
    )
    delta = jnp.transpose(jnp.sum(upstream_gradient.astype(jnp.float32) * attended, -1), (1, 2, 0))[
        ..., None
    ]
    score_gradient = (probs * (dprobs - delta) * scale).astype(jnp.bfloat16)
    dquery = (
        jnp.einsum(
            "gnst,tgd->sgnd", score_gradient, key_projected, preferred_element_type=jnp.float32
        )
        .reshape(sequence_length, query_columns)
        .astype(jnp.bfloat16)
    )
    key_gradient = (
        jnp.einsum("xoil,ixoy->lxy", score_gradient, query_four, preferred_element_type=jnp.float32)
        .reshape(sequence_length, key_value_columns)
        .astype(jnp.bfloat16)
    )
    dvalue_low = value_gradient.reshape(sequence_length, key_value_columns).astype(jnp.bfloat16)
    grad_cols = jnp.concatenate([dquery, key_gradient, dvalue_low], 1)
    term = lax.dot_general(
        grad_cols, gathered, (((1,), (1,)), ((), ())), preferred_element_type=jnp.float32
    )
    input_grad = lax.psum_scatter(term, "tensor", scatter_dimension=1, tiled=True).astype(
        jnp.bfloat16
    )
    owned = lax.psum_scatter(
        jnp.einsum(
            "sabc,sn->bacn", inputs_four, grad_cols, preferred_element_type=jnp.float32
        ).astype(jnp.bfloat16),
        "dp",
        scatter_dimension=0,
        tiled=True,
    ).astype(jnp.float32)
    gradient = jnp.transpose(owned, (1, 0, 2, 3))
    new_weights, new_first, new_second = adam_update(relaid, gradient, moved_first, moved_second)
    return (input_grad, new_weights, new_first, new_second)


def solution(mesh):
    return jax.shard_map(
        local,
        mesh=mesh,
        in_specs=(
            P("dp", None),
            P("dp", "tensor"),
            P("dp"),
            P("tensor", None, None, "dp"),
            P("tensor", None, None, "dp"),
            P("tensor", None, None, "dp"),
        ),
        out_specs=(
            P("dp", "tensor"),
            P(None, "dp", None, "tensor"),
            P(None, "dp", None, "tensor"),
            P(None, "dp", None, "tensor"),
        ),
        check_vma=False,
    )
```

profile of v0, /device:TPU:0, one launch (start us, length us, event | category | flops | bytes accessed | tf_op | source)
XLA Modules:
  0.0 1028.4 jit_solution(11852755882818706069)
XLA Ops:
  7.2 3.2 copy.71
  10.4 42.8 %all_to_all.90 = bf16[1,8,256,768]{2,3,0,1:T(8,128)(2,1)S(1)} all-to-all(bf16[1,8,256,768]{2,3,0,1:T(8,128)(2,1)S(1)} %copy.71), channel_id=1, replica_groups=mesh['dp'=8,'tensor'=4] {'dp'}, dimensions={1} | all-to-all | bytes 6291456 | tf_op jit(solution)/shard_map/all_to_all | solution.py:35
  53.2 37.1 %copy.128 = bf16[1,1,256,6144]{2,1,0,3:T(2,128)(2,1)} copy(bf16[1,1,256,6144]{2,3,1,0:T(8,128)(2,1)S(1)} %bitcast.135) | data formatting | bytes 6291456 | tf_op jit(solution)/shard_map/all_to_all | solution.py:35
  90.8 33.2 %reduce = bf16[6144,256]{1,0:T(8,128)(2,1)} reduce(bf16[6144,1,1,256]{3,2,1,0:T(2,128)(2,1)} %bitcast.133, bf16[]{:T(256)} %broadcast.138), dimensions={1,2}, to_apply=%bitcast.124.reduce_sub_computation | reduce | bytes 6291458
  127.0 74.9 %all_to_all.91 = bf16[4,2,196608]{2,1,0:T(2,128)(2,1)} all-to-all(bf16[4,2,196608]{2,1,0:T(2,128)(2,1)S(1)} %reshape.214), channel_id=1, replica_groups=mesh['dp'=8,'tensor'=4] {'tensor'}, dimensions={0} | all-to-all | bytes 6291456 | tf_op jit(solution)/shard_map/all_to_all | solution.py:34
  201.9 6.1 reshape.215
  208.0 3.3 copy.120
  214.1 6.8 copy.87
  220.9 4.9 all-to-all-start.2
  228.8 5.6 copy.122
  235.1 169.6 %all-gather.3.cloned.1.call-done = bf16[4,8,1,256,1536]{4,3,2,0,1:T(8,128)(2,1)} async-done(((bf16[4,1,1,256,1536]{4,3,2,0,1:T(8,128)(2,1)}), bf16[4,8,1,256,1536]{4,3,2,0,1:T(8,128)(2,1)}) %all-gather.3.cloned.1.call-update) | async-done | bytes 25165840 | tf_op jit(solution)/shard_map/all_gather | solution.py:63
  404.7 21.0 %copy.74 = bf16[4,8,1,256,1536]{4,3,1,0,2:T(8,128)(2,1)} copy(bf16[4,8,1,256,1536]{4,3,2,0,1:T(8,128)(2,1)} %all-gather.3.cloned.1.call-done) | data formatting | bytes 50331648 | tf_op jit(solution)/shard_map/all_gather | solution.py:63
  425.6 11.7 %convolution_convert_fusion = bf16[256,1536]{1,0:T(8,128)(2,1)S(1)} fusion(bf16[256,8192]{1,0:T(8,128)(2,1)S(1)} %copy-done, bf16[8192,1536]{1,0:T(8,128)(2,1)} %bitcast.129), kind=kOutput, calls=%fused_computation.15 | convolution fusion | flops 6442844160 | bytes 30146560 | tf_op jit(solution)/shard_map/dot_general | solution.py:64
  440.6 3.2 fusion.36
  451.4 13.6 %convert_bitcast_fusion = bf16[8,4,256,1536]{2,3,0,1:T(8,128)(2,1)} fusion(bf16[256,4,8,256]{3,2,1,0:T(8,128)(2,1)} %bitcast.126, bf16[256,256]{0,1:T(8,128)(2,1)S(1)} %bitcast.148, bf16[256,256]{0,1:T(8,128)(2,1)S(1)} %bitcast.141, bf16[256,1024]{0,1:T(8,128)(2,1)} %bitcast.137), kind=kOutput, calls=%fused_computation.1 | convolution fusion | flops 6457393152 | bytes 30146560 | tf_op jit(solution)/shard_map/sabc,sn->bacn/dot_general | solution.py:131
  465.1 6.8 copy.92
  471.9 4.7 all-to-all-start.4
  476.6 8.5 copy.88
  485.1 112.1 %all-to-all-done.4 = f32[1,8,256,768]{2,3,0,1:T(8,128)} async-done(((f32[1,8,256,768]{2,3,0,1:T(8,128)}), f32[1,8,256,768]{2,3,0,1:T(8,128)}, u32[]{:S(2)}, u32[]{:S(2)}) %all-to-all-start.4) | async-done | bytes 6291488 | tf_op jit(solution)/shard_map/all_to_all | solution.py:55
  597.2 5.5 all-to-all-start.3
  602.8 14.1 %fusion.22 = f32[256,8192]{1,0:T(8,128)} fusion(bf16[8192,1536]{1,0:T(8,128)(2,1)} %bitcast.130, bf16[256,256]{0,1:T(8,128)(2,1)S(1)} %bitcast.149, bf16[256,256]{0,1:T(8,128)(2,1)S(1)} %bitcast.142, bf16[256,1024]{0,1:T(8,128)(2,1)} %bitcast.138), kind=kOutput, calls=%fused_computation.40 | convolution fusion | flops 6444810240 | bytes 34340864 | tf_op jit(solution)/shard_map/dot_general | solution.py:124
  616.9 8.6 copy.93
  625.5 116.1 %all-to-all-done.3 = f32[1,1,256,6144]{2,1,0,3:T(1,128)} async-done(((f32[1,1,256,6144]{2,1,0,3:T(1,128)}), f32[1,1,256,6144]{2,1,0,3:T(1,128)}, u32[]{:S(2)}, u32[]{:S(2)}) %all-to-all-start.3) | async-done | bytes 6291488 | tf_op jit(solution)/shard_map/all_to_all | solution.py:47
  741.6 5.3 all-to-all-start.5
  747.6 6.3 copy_multiply_fusion.1
  753.9 209.1 %all-to-all-done.5 = f32[1,1,256,6144]{2,1,0,3:T(1,128)} async-done(((f32[1,1,256,6144]{2,1,0,3:T(1,128)}), f32[1,1,256,6144]{2,1,0,3:T(1,128)}, u32[]{:S(2)}, u32[]{:S(2)}) %all-to-all-start.5) | async-done | bytes 6291488 | tf_op jit(solution)/shard_map/all_to_all | solution.py:54
  963.0 6.2 copy_multiply_fusion
  969.2 12.6 %fusion.3 = (bf16[4,1,256,1536]{2,3,0,1:T(8,128)(2,1)}, f32[4,1,256,1536]{2,3,0,1:T(8,128)}, f32[4,1,256,1536]{2,3,0,1:T(8,128)}) fusion(bf16[4,1,256,1536]{2,3,0,1:T(8,128)(2,1)S(1)} %bitcast.128, f32[4,1,256,1536]{2,3,0,1:T(8,128)} %bitcast.131, bf16[8,4,256,1536]{2,3,0,1:T(8,128)(2,1)} %all-reduce.3.cloned.1.call-done, u32[]{:T(128)} %bitcast.64, ...), kind=kLoop, calls=%fused_computation.9 | loop fusion | flops 25165824 | bytes 34603012 | tf_op jit(solution)/shard_map/convert_element_type | solution.py:25
  981.7 4.6 copy.95
  986.4 6.6 copy.96
  992.9 6.6 copy.97
  999.5 19.6 %reduce-scatter.5.cloned.1.call-done = f32[256,2048]{1,0:T(8,128)} async-done(((f32[256,8192]{1,0:T(8,128)}), f32[256,2048]{1,0:T(8,128)}) %reduce-scatter.5.cloned.1.call-update) | async-done | bytes 2097168 | tf_op jit(solution)/shard_map/reduce_scatter | solution.py:127
  (37 shorter events, 23.6 us)
Async XLA Ops:
  7.2 397.5 %all-gather.3.cloned.1.call-start = ((), (), s32[]{:S(2)}) async-start(), calls=%async_computation.8 | async-start | bytes 28311552 | tf_op jit(solution)/shard_map/all_gather | solution.py:63
  220.9 250.9 %all-to-all-start.2 = ((f32[1,8,256,768]{2,3,0,1:T(8,128)}), f32[1,8,256,768]{2,3,0,1:T(8,128)}, u32[]{:S(2)}, u32[]{:S(2)}) async-start(f32[1,8,256,768]{2,3,0,1:T(8,128)} %copy.87), calls=%async_computation.3 | async-start | bytes 12582912 | tf_op jit(solution)/shard_map/all_to_all | solution.py:48
  225.8 743.4 %all-reduce.3.cloned.1.call-start = ((), (), s32[]{:S(2)}) async-start(), calls=%async_computation.9 | async-start | bytes 50331648
  404.7 21.0 %copy-start = (bf16[256,8192]{1,0:T(8,128)(2,1)S(1)}, bf16[256,8192]{1,0:T(8,128)(2,1)}, u32[]{:S(2)}) copy-start(bf16[256,8192]{1,0:T(8,128)(2,1)} %param.6) | copy-start | bytes 12582916
  445.5 3.8 copy-start.1
  447.0 4.0 copy-start.2
  471.9 125.4 %all-to-all-start.4 = ((f32[1,8,256,768]{2,3,0,1:T(8,128)}), f32[1,8,256,768]{2,3,0,1:T(8,128)}, u32[]{:S(2)}, u32[]{:S(2)}) async-start(f32[1,8,256,768]{2,3,0,1:T(8,128)} %copy.92), calls=%async_computation.5 | async-start | bytes 12582912 | tf_op jit(solution)/shard_map/all_to_all | solution.py:55
  597.2 144.4 %all-to-all-start.3 = ((f32[1,1,256,6144]{2,1,0,3:T(1,128)}), f32[1,1,256,6144]{2,1,0,3:T(1,128)}, u32[]{:S(2)}, u32[]{:S(2)}) async-start(f32[1,1,256,6144]{2,1,0,3:T(1,128)} %copy.88), calls=%async_computation.4 | async-start | bytes 12582912 | tf_op jit(solution)/shard_map/all_to_all | solution.py:47
  602.7 416.4 %reduce-scatter.5.cloned.1.call-start = ((), (), s32[]{:S(2)}) async-start(), calls=%async_computation.7 | async-start | bytes 10485760 | tf_op jit(solution)/shard_map/reduce_scatter | solution.py:127
  625.5 121.5 %copy-start.3 = (u32[32]{0:T(128)S(1)}, u32[32]{0:T(128)}, u32[]{:S(2)}) copy-start(u32[32]{0:T(128)} %constant.30) | copy-start | bytes 388
  741.6 221.4 %all-to-all-start.5 = ((f32[1,1,256,6144]{2,1,0,3:T(1,128)}), f32[1,1,256,6144]{2,1,0,3:T(1,128)}, u32[]{:S(2)}, u32[]{:S(2)}) async-start(f32[1,1,256,6144]{2,1,0,3:T(1,128)} %copy.93), calls=%async_computation.6 | async-start | bytes 12582912 | tf_op jit(solution)/shard_map/all_to_all | solution.py:54
Sparse Core Ops, SparseCore 0:
  214.3 190.3 all-gather.2
  465.2 374.4 all-reduce.2
  842.2 176.9 reduce-scatter.4
where the time goes:
time: 1030 us
  waiting for transfers between devices  627 us (61%)
  local copies, waits for them, and re-layouts  137 us (13%)
  blocking collectives  118 us (11%)
  other arithmetic  63.5 us (6%)
  matrix products  48.4 us (5%)
  starting transfers between devices  20.7 us (2%)
  between operations  14.6 us (1%)
    all_to_all x1, waiting for transfers between devices, local(): lax.all_to_all(lax.all_to_all(moment2, 'dp', split_axis=1, concat_axis=3,...  209 us
    all_gather x1, waiting for transfers between devices, local(): lax.all_gather(relaid, 'dp', axis=1, tiled=True).reshape(width, block_cols)  170 us
    all_to_all x1, waiting for transfers between devices, local(): lax.all_to_all(lax.all_to_all(moment1, 'dp', split_axis=1, concat_axis=3,...  116 us
    all_to_all x1, waiting for transfers between devices, local(): lax.all_to_all(moment2, 'dp', split_axis=1, concat_axis=3, tiled=True)  112 us
    all_to_all x1, blocking collectives, local(): lax.all_to_all(lax.all_to_all(weights, 'dp', split_axis=1, concat_axis=3,...  74.9 us
    unnamed x21, local copies, waits for them, and re-layouts  55.7 us
    all_to_all x1, blocking collectives, local(): lax.all_to_all(weights, 'dp', split_axis=1, concat_axis=3, tiled=True)  42.8 us
    all_to_all x1, local copies, waits for them, and re-layouts, local(): lax.all_to_all(weights, 'dp', split_axis=1, concat_axis=3, tiled=True)  37.1 us
  transfers between devices with their start and end apart: 7, of which 5 were waited for; matrix products, arithmetic and copies ran while one was open for 15% of the time, Pallas kernels for 0%

commit v1 on v0

v1 whole, which is shorter than its diff:
```python
import functools

import jax
import jax.numpy as jnp
from jax import lax
from jax.experimental import pallas as pl
from jax.experimental.pallas import tpu as pltpu
from jax.sharding import PartitionSpec as P

QUERY_HEADS = 32
KEY_VALUE_HEADS = 8
HEAD_SIZE = 128


beta_first = 0.9
beta_second = 0.95
adam_eps = 1e-08
learn_rate = 0.002
decay_rate = 0.1
bias_first = 1.0 - beta_first**20
bias_second = 1.0 - beta_second**20

MIB = 1 << 20
VMEM = pl.BlockSpec(memory_space=pltpu.VMEM)
SMEM = pl.BlockSpec(memory_space=pltpu.SMEM)


def adam_update(param, gradient, first, second):
    first_new = beta_first * first + (1.0 - beta_first) * gradient
    second_new = beta_second * second + (1.0 - beta_second) * gradient * gradient
    ratio = first_new / bias_first / (jnp.sqrt(second_new / bias_second) + adam_eps)
    widened = param.astype(jnp.float32)
    updated = (widened - learn_rate * (ratio + decay_rate * widened)).astype(jnp.bfloat16)
    return (updated, first_new, second_new)


def shape_of(dims, dtype=jnp.bfloat16):
    return jax.ShapeDtypeStruct(dims, dtype)


def size_of(arrays):
    return sum(a.size * a.dtype.itemsize for a in arrays)


def whole_call(body, outs, ins, name, flops=0, scalars=1):
    moved = size_of(ins[scalars:]) + size_of(outs)
    return pl.pallas_call(
        body,
        out_shape=outs,
        in_specs=[SMEM] * scalars + [VMEM] * (len(ins) - scalars),
        out_specs=[VMEM] * len(outs),
        compiler_params=pltpu.CompilerParams(vmem_limit_bytes=int(1.3 * moved) + 12 * MIB),
        cost_estimate=pl.CostEstimate(flops=flops, bytes_accessed=moved, transcendentals=0),
        name=name,
    )(*ins)


def after(x, *others):
    return lax.optimization_barrier((x,) + others)[0]


def pack_blocks(me, blocks):
    count = blocks.shape[0]

    def body(me_ref, in_ref, *out_refs):
        for k in range(count):
            out_refs[k][...] = in_ref[me_ref[0] ^ k].astype(jnp.bfloat16)

    return whole_call(body, [shape_of(blocks.shape[1:])] * count, [me, blocks], "pack_blocks")


def place_blocks(me, pieces):
    count = len(pieces)

    def body(me_ref, *refs):
        for k in range(count):
            refs[count][me_ref[0] ^ k] = refs[k][...]

    return whole_call(body, [shape_of((count,) + pieces[0].shape)], [me, *pieces], "place_blocks")[0]


def pack_columns(me, tokens, tensor_count, replica_count):
    length, width = tokens.shape
    rows = width // (tensor_count * replica_count)
    dims = (length, tensor_count * rows)
    if rows % 128:
        parts = tokens.reshape(length, tensor_count, replica_count, rows).transpose(2, 0, 1, 3)
        return [lax.dynamic_index_in_dim(parts, me[0] ^ k, 0, False).reshape(dims) for k in range(replica_count)]

    def body(me_ref, in_ref, *out_refs):
        for k in range(replica_count):
            for t in range(tensor_count):
                start = pl.multiple_of((t * replica_count + (me_ref[0] ^ k)) * rows, rows)
                out_refs[k][:, t * rows : (t + 1) * rows] = in_ref[:, pl.ds(start, rows)]

    return whole_call(body, [shape_of(dims)] * replica_count, [me, tokens], "pack_columns")


def place_columns(me, pieces):
    count = len(pieces)
    length, rows = pieces[0].shape
    if rows % 128:
        stacked = place_blocks(me, pieces)
        return stacked.transpose(1, 0, 2).reshape(length, count * rows)

    def body(me_ref, *refs):
        for k in range(count):
            start = pl.multiple_of((me_ref[0] ^ k) * rows, rows)
            refs[count][:, pl.ds(start, rows)] = refs[k][...]

    return whole_call(body, [shape_of((length, count * rows))], [me, *pieces], "place_columns")[0]


def swap(x, k):
    if k == 0:
        return x
    return lax.ppermute(x, "dp", [(i, i ^ k) for i in range(lax.axis_size("dp"))])


def exchange(pieces):
    return [swap(piece, k) for k, piece in enumerate(pieces)]


def over_tensor(x):
    return lax.all_to_all(x, "tensor", split_axis=0, concat_axis=0, tiled=True)


def project(pieces, weight, received=None):
    rows, depth = pieces[0].shape
    parts, columns = weight.shape[1], weight.shape[3]
    count = len(pieces)
    extra = [] if received is None else [received]
    dims = (rows, parts * columns)
    outs = [shape_of((count,) + dims)] if received is None else [shape_of(dims)] * count

    def body(*refs):
        weight_ref = refs[count]
        out_refs = refs[count + 1 + len(extra) :]
        for e in range(parts):
            block = weight_ref[:, e].reshape(depth, columns)
            cut = slice(e * columns, (e + 1) * columns)
            for k in range(count):
                value = jnp.dot(refs[k][...], block, preferred_element_type=jnp.float32)
                if received is None:
                    out_refs[0][k, :, cut] = value.astype(jnp.bfloat16)
                else:
                    value = value + refs[count + 1][k, :, cut].astype(jnp.float32)
                    out_refs[k][:, cut] = value.astype(jnp.bfloat16)

    flops = 2 * count * rows * depth * parts * columns
    return whole_call(body, outs, [*pieces, weight, *extra], "project", flops, 0)


def attention(length, terms, upstream):
    count = len(terms)
    rows, columns = terms[0].shape
    query_columns = upstream.shape[1]
    key_value_columns = (columns - query_columns) // 2
    heads = key_value_columns // HEAD_SIZE
    group = QUERY_HEADS // KEY_VALUE_HEADS
    scale = HEAD_SIZE ** (-0.5)

    def body(length_ref, *refs):
        upstream_ref, out_ref = refs[count], refs[count + 1]

        def projected(start):
            cut = slice(start, start + HEAD_SIZE)
            total = refs[0][:, cut].astype(jnp.float32)
            for term in refs[1:count]:
                total = total + term[:, cut].astype(jnp.float32)
            return total.astype(jnp.bfloat16)

        def dot(a, b, on_a, on_b):
            return lax.dot_general(a, b, (((on_a,), (on_b,)), ((), ())), preferred_element_type=jnp.float32)

        live = length_ref[0]
        at = lax.broadcasted_iota(jnp.int32, (rows, rows), 0)
        of = lax.broadcasted_iota(jnp.int32, (rows, rows), 1)
        allowed = (of <= at) & (of < live)
        active = lax.broadcasted_iota(jnp.int32, (rows, HEAD_SIZE), 0) < live
        for g in range(heads):
            key_start = query_columns + g * HEAD_SIZE
            value_start = query_columns + key_value_columns + g * HEAD_SIZE
            key, value = projected(key_start), projected(value_start)
            key_gradient = jnp.zeros((rows, HEAD_SIZE), jnp.float32)
            value_gradient = jnp.zeros((rows, HEAD_SIZE), jnp.float32)
            for n in range(group):
                start = (g * group + n) * HEAD_SIZE
                query = projected(start)
                given = upstream_ref[:, start : start + HEAD_SIZE]
                given = jnp.where(active, given, jnp.zeros_like(given))
                scores = jnp.where(allowed, dot(query, key, 1, 1) * scale, -jnp.inf)
                expo = jnp.exp(scores - jnp.max(scores, -1, keepdims=True))
                probs = expo / jnp.sum(expo, -1, keepdims=True)
                low = probs.astype(jnp.bfloat16)
                attended = dot(low, value, 1, 0)
                delta = jnp.sum(given.astype(jnp.float32) * attended, -1, keepdims=True)
                score_gradient = (probs * (dot(given, value, 1, 1) - delta) * scale).astype(jnp.bfloat16)
                out_ref[:, start : start + HEAD_SIZE] = dot(score_gradient, key, 1, 0).astype(jnp.bfloat16)
                key_gradient = key_gradient + dot(score_gradient, query, 0, 0)
                value_gradient = value_gradient + dot(low, given, 0, 0)
            out_ref[:, key_start : key_start + HEAD_SIZE] = key_gradient.astype(jnp.bfloat16)
            out_ref[:, value_start : value_start + HEAD_SIZE] = value_gradient.astype(jnp.bfloat16)

    flops = 2 * heads * group * 6 * rows * rows * HEAD_SIZE
    return whole_call(body, [shape_of((rows, columns))], [length, *terms, upstream], "attention", flops)[0]


def input_terms(columns, weight):
    tensor_count, parts, width, cut_columns = weight.shape
    count = len(columns)
    rows = columns[0].shape[0]

    def body(*refs):
        weight_ref, out_ref = refs[count], refs[count + 1]
        for k in range(count):
            total = None
            for e in range(parts):
                block = weight_ref[:, e].reshape(tensor_count * width, cut_columns)
                term = lax.dot_general(
                    refs[k][:, e * cut_columns : (e + 1) * cut_columns],
                    block,
                    (((1,), (1,)), ((), ())),
                    preferred_element_type=jnp.float32,
                )
                total = term if total is None else total + term
            for t in range(tensor_count):
                out_ref[t, k] = total[:, t * width : (t + 1) * width].astype(jnp.bfloat16)

    flops = 2 * count * rows * tensor_count * width * parts * cut_columns
    outs = [shape_of((tensor_count, count, rows, width))]
    return whole_call(body, outs, [*columns, weight], "input_terms", flops, 0)[0]


def sum_terms(terms):
    tensor_count, count, rows, width = terms.shape

    def body(in_ref, *out_refs):
        for k in range(count):
            total = in_ref[0, k].astype(jnp.float32)
            for t in range(1, tensor_count):
                total = total + in_ref[t, k].astype(jnp.float32)
            out_refs[k][...] = total.astype(jnp.bfloat16)

    return whole_call(body, [shape_of((rows, width))] * count, [terms], "sum_terms", 0, 0)


def update(pieces, columns, weight, first, second):
    tensor_count, parts, width, cut_columns = weight.shape
    count = len(pieces)
    rows = pieces[0].shape[0]
    dims = (tensor_count, 1, width, parts * cut_columns)
    if width % 128:
        inputs = jnp.concatenate(pieces, 0)
        gradient = lax.dot_general(
            inputs, jnp.concatenate(columns, 0), (((0,), (0,)), ((), ())), preferred_element_type=jnp.float32
        ).reshape(dims)
        merged = [a.transpose(0, 2, 1, 3).reshape(dims) for a in (weight, first, second)]
        return adam_update(merged[0], gradient, merged[1].astype(jnp.float32), merged[2].astype(jnp.float32))

    def body(*refs):
        weight_ref, first_ref, second_ref, new_weight, new_first, new_second = refs[2 * count :]
        gradient = None
        for k in range(count):
            term = lax.dot_general(
                refs[k][...], refs[count + k][...], (((0,), (0,)), ((), ())), preferred_element_type=jnp.float32
            )
            gradient = term if gradient is None else gradient + term
        updated, moved_first, moved_second = adam_update(
            weight_ref[0, 0],
            gradient,
            first_ref[0, 0].astype(jnp.float32),
            second_ref[0, 0].astype(jnp.float32),
        )
        new_weight[0, 0] = updated
        new_first[0, 0] = moved_first
        new_second[0, 0] = moved_second

    old = pl.BlockSpec((1, 1, width, cut_columns), lambda e, t: (t, e, 0, 0))
    new = pl.BlockSpec((1, 1, width, cut_columns), lambda e, t: (t, 0, 0, e))
    outs = [shape_of(dims), shape_of(dims, jnp.float32), shape_of(dims, jnp.float32)]
    ins = [*pieces, *columns, weight, first, second]
    return pl.pallas_call(
        body,
        grid=(parts, tensor_count),
        out_shape=outs,
        in_specs=[pl.BlockSpec((rows, width), lambda e, t: (0, t))] * count
        + [pl.BlockSpec((rows, cut_columns), lambda e, t: (0, e))] * count
        + [old] * 3,
        out_specs=[new] * 3,
        compiler_params=pltpu.CompilerParams(vmem_limit_bytes=40 * MIB),
        cost_estimate=pl.CostEstimate(
            flops=2 * count * rows * tensor_count * width * parts * cut_columns,
            bytes_accessed=size_of(ins) + size_of(outs),
            transcendentals=0,
        ),
        name="update",
    )(*ins)


def local(tokens, grad_out, lengths, weights, moment1, moment2):
    tensor_count = lax.axis_size("tensor")
    replica_count = lax.axis_size("dp")
    width, cut_columns = weights.shape[2:]
    parts = replica_count // tensor_count
    me = lax.axis_index("dp").astype(jnp.int32).reshape(1)
    new_split = (tensor_count, parts, width, cut_columns)

    weight_pieces = exchange(pack_blocks(me, weights[0]))
    weight_rows = place_blocks(me, weight_pieces)
    weight = over_tensor(weight_rows).reshape(new_split)

    token_pieces = exchange(pack_columns(me, tokens, tensor_count, replica_count))

    first_rows = place_blocks(me, exchange(pack_blocks(me, after(moment1[0], weight_rows))))
    first = over_tensor(first_rows).reshape(new_split)
    second_rows = place_blocks(me, exchange(pack_blocks(me, after(moment2[0], weight))))
    second = over_tensor(second_rows).reshape(new_split)

    sent = project(token_pieces[1::2], weight)[0]
    sums = project(token_pieces[0::2], weight, swap(sent, 1))
    terms = [swap(term, 2 * m) for m, term in enumerate(sums)]
    columns = attention(lengths, terms, grad_out)

    same_core = [swap(columns, 2 * m) for m in range(replica_count // 2)]
    other_core = [swap(x, 1) for x in same_core]
    all_columns = [x for pair in zip(same_core, other_core) for x in pair]

    moved = over_tensor(input_terms(all_columns, weight))
    input_grad = place_columns(me, exchange(sum_terms(moved)))
    new_weights, new_first, new_second = update(token_pieces, all_columns, weight, first, second)
    return (input_grad, new_weights, new_first, new_second)


def solution(mesh):
    return jax.shard_map(
        local,
        mesh=mesh,
        in_specs=(
            P("dp", None),
            P("dp", "tensor"),
            P("dp"),
            P("tensor", None, None, "dp"),
            P("tensor", None, None, "dp"),
            P("tensor", None, None, "dp"),
        ),
        out_specs=(
            P("dp", "tensor"),
            P(None, "dp", None, "tensor"),
            P(None, "dp", None, "tensor"),
            P(None, "dp", None, "tensor"),
        ),
        check_vma=False,
    )
```

time: 1030 us -> 517 us (0.50)
  waiting for transfers between devices: 627 us -> 351 us
  blocking collectives: 118 us -> 0 us
  local copies, waits for them, and re-layouts: 137 us -> 45.8 us
  other arithmetic: 63.5 us -> 0.01 us
  Pallas kernels: 0 us -> 52.4 us
  matrix products: 48.4 us -> 0 us
  starting transfers between devices: 20.7 us -> 64.7 us
  between operations: 14.6 us -> 1.56 us
    all_to_all x4, waiting for transfers between devices: 437 us -> 148 us  [over_tensor(): return lax.all_to_all(x, 'tensor', split_axis=0, concat_axis=0, tiled=True)]
    ppermute x0 -> x46, waiting for transfers between devices: none -> 203 us  [swap(): lax.ppermute(x, 'dp', [(i, i ^ k) for i in range(lax.axis_size('dp'))])]
    all_gather x1 -> x0, waiting for transfers between devices: 170 us -> none  [local(): lax.all_gather(relaid, 'dp', axis=1, tiled=True).reshape(width, block_cols)]
    all_to_all x2 -> x0, blocking collectives: 118 us -> none  [the longest x1 74.9 us: local(): lax.all_to_all(lax.all_to_all(weights, 'dp', split_axis=1, concat_axis=3,...]
    all_to_all x4 -> x0, local copies, waits for them, and re-layouts: 57 us -> none  [the longest x1 37.1 us: local(): lax.all_to_all(weights, 'dp', split_axis=1, concat_axis=3, tiled=True)]
    pallas_call x0 -> x14, Pallas kernels: none -> 52.4 us  [the longest x13 35.4 us: whole_call(): pl.pallas_call(body, out_shape=outs, in_specs=[SMEM] * scalars + [VMEM] *...]
    dot_general x8 -> x0, matrix products: 45.2 us -> none  [the longest x1 14.1 us: local(): lax.dot_general(grad_cols, gathered, (((1,), (1,)), ((), ())), preferred_...]
    ppermute x0 -> x46, starting transfers between devices: none -> 45 us  [swap(): lax.ppermute(x, 'dp', [(i, i ^ k) for i in range(lax.axis_size('dp'))])]
  transfers between devices with their start and end apart: 7 -> 50, of which waited for: 5 -> 25; matrix products, arithmetic and copies ran while one was open for 15% -> 0% of each run, Pallas kernels for 0% -> 8%
where the time goes in v1:
time: 517 us; the launch traced here: 516 us
  waiting for transfers between devices  351 us (68%)
  starting transfers between devices  64.7 us (13%)
  Pallas kernels  52.4 us (10%)
  local copies, waits for them, and re-layouts  45.8 us (9%)
    ppermute x46, waiting for transfers between devices, swap(): lax.ppermute(x, 'dp', [(i, i ^ k) for i in range(lax.axis_size('dp'))])  203 us
    all_to_all x4, waiting for transfers between devices, over_tensor(): return lax.all_to_all(x, 'tensor', split_axis=0, concat_axis=0, tiled=True)  148 us
    unnamed x94, local copies, waits for them, and re-layouts  45.8 us
    ppermute x46, starting transfers between devices, swap(): lax.ppermute(x, 'dp', [(i, i ^ k) for i in range(lax.axis_size('dp'))])  45 us
    pallas_call x13, Pallas kernels, whole_call(): pl.pallas_call(body, out_shape=outs, in_specs=[SMEM] * scalars + [VMEM] *...  35.4 us
    all_to_all x4, starting transfers between devices, over_tensor(): return lax.all_to_all(x, 'tensor', split_axis=0, concat_axis=0, tiled=True)  19.6 us
    pallas_call x1, Pallas kernels, update(): pl.pallas_call(body, grid=(parts, tensor_count), out_shape=outs, in_specs...  17 us
  transfers between devices with their start and end apart: 50, of which 25 were waited for; matrix products, arithmetic and copies ran while one was open for 0% of the time, Pallas kernels for 8%

profile of v1, /device:TPU:0, one launch (start us, length us, event | category | flops | bytes accessed | tf_op | source)
XLA Modules:
  0.0 515.8 jit_solution(2113319849091501526)
XLA Ops:
  10.3 5.5 %collective-permute-done.4.refs_2_ = bf16[256,768]{1,0:T(8,128)(2,1)S(1)} collective-permute-done((bf16[256,768]{1,0:T(8,128)(2,1)S(1)}, bf16[256,768]{1,0:T(8,128)(2,1)S(1)}, u32[]{:S(2)}, u32[]{:S(2)}) %collective-permute-start.4) | collective-permute-done | bytes 393248 | tf_op jit(solution)/shard_map/ppermute | solution.py:117
  17.5 6.2 %collective-permute-done.5.refs_3_ = bf16[256,768]{1,0:T(8,128)(2,1)S(1)} collective-permute-done((bf16[256,768]{1,0:T(8,128)(2,1)S(1)}, bf16[256,768]{1,0:T(8,128)(2,1)S(1)}, u32[]{:S(2)}, u32[]{:S(2)}) %collective-permute-start.5) | collective-permute-done | bytes 393248 | tf_op jit(solution)/shard_map/ppermute | solution.py:117
  23.7 18.1 %collective-permute-done.7.refs_5_ = bf16[256,768]{1,0:T(8,128)(2,1)S(1)} collective-permute-done((bf16[256,768]{1,0:T(8,128)(2,1)S(1)}, bf16[256,768]{1,0:T(8,128)(2,1)S(1)}, u32[]{:S(2)}, u32[]{:S(2)}) %collective-permute-start.7) | collective-permute-done | bytes 393248 | tf_op jit(solution)/shard_map/ppermute | solution.py:117
  43.7 5.3 %all-to-all-start = ((bf16[8,256,768]{2,1,0:T(8,128)(2,1)}), bf16[8,256,768]{2,1,0:T(8,128)(2,1)S(1)}, u32[]{:S(2)}, u32[]{:S(2)}) async-start(bf16[8,256,768]{2,1,0:T(8,128)(2,1)} %place_blocks.3), calls=%async_computation | async-start | bytes 6291456 | tf_op jit(solution)/shard_map/all_to_all | solution.py:125
  59.1 9.7 %collective-permute-done.11.refs_1_.refs_3_ = bf16[256,1024]{1,0:T(8,128)(2,1)S(1)} collective-permute-done((bf16[256,1024]{1,0:T(8,128)(2,1)S(1)}, bf16[256,1024]{1,0:T(8,128)(2,1)S(1)}, u32[]{:S(2)}, u32[]{:S(2)}) %collective-permute-start.11) | collective-permute-done | bytes 524320 | tf_op jit(solution)/shard_map/ppermute | solution.py:117
  69.6 12.2 %collective-permute-done.12.refs_2_.refs_5_ = bf16[256,1024]{1,0:T(8,128)(2,1)S(1)} collective-permute-done((bf16[256,1024]{1,0:T(8,128)(2,1)S(1)}, bf16[256,1024]{1,0:T(8,128)(2,1)S(1)}, u32[]{:S(2)}, u32[]{:S(2)}) %collective-permute-start.12) | collective-permute-done | bytes 524320 | tf_op jit(solution)/shard_map/ppermute | solution.py:117
  83.4 36.8 %all-to-all-done = bf16[8,256,768]{2,1,0:T(8,128)(2,1)S(1)} async-done(((bf16[8,256,768]{2,1,0:T(8,128)(2,1)}), bf16[8,256,768]{2,1,0:T(8,128)(2,1)S(1)}, u32[]{:S(2)}, u32[]{:S(2)}) %all-to-all-start) | async-done | bytes 3145760 | tf_op jit(solution)/shard_map/all_to_all | solution.py:125
  124.7 5.1 project.2
  137.3 5.4 %collective-permute-done.33.refs_2_ = bf16[256,768]{1,0:T(8,128)(2,1)S(1)} collective-permute-done((bf16[256,768]{1,0:T(8,128)(2,1)S(1)}, bf16[256,768]{1,0:T(8,128)(2,1)S(1)}, u32[]{:S(2)}, u32[]{:S(2)}) %collective-permute-start.33) | collective-permute-done | bytes 393248 | tf_op jit(solution)/shard_map/ppermute | solution.py:117
  145.1 5.0 collective-permute-done.34.refs_3_
  150.1 3.2 collective-permute-start.38
  153.3 15.6 %collective-permute-done.36.refs_5_ = bf16[256,768]{1,0:T(8,128)(2,1)S(1)} collective-permute-done((bf16[256,768]{1,0:T(8,128)(2,1)S(1)}, bf16[256,768]{1,0:T(8,128)(2,1)S(1)}, u32[]{:S(2)}, u32[]{:S(2)}) %collective-permute-start.36) | collective-permute-done | bytes 393248 | tf_op jit(solution)/shard_map/ppermute | solution.py:117
  170.7 4.8 all-to-all-start.2
  179.1 11.5 %collective-permute-done.refs_1_.refs_2_ = bf16[256,1024]{1,0:T(8,128)(2,1)S(1)} collective-permute-done((bf16[256,1024]{1,0:T(8,128)(2,1)}, bf16[256,1024]{1,0:T(8,128)(2,1)S(1)}, u32[]{:S(2)}, u32[]{:S(2)}) %collective-permute-start) | collective-permute-done | bytes 524320 | tf_op jit(solution)/shard_map/ppermute | solution.py:117
  190.6 11.7 %collective-permute-done.1.refs_2_.refs_4_ = bf16[256,1024]{1,0:T(8,128)(2,1)S(1)} collective-permute-done((bf16[256,1024]{1,0:T(8,128)(2,1)}, bf16[256,1024]{1,0:T(8,128)(2,1)S(1)}, u32[]{:S(2)}, u32[]{:S(2)}) %collective-permute-start.1) | collective-permute-done | bytes 524320 | tf_op jit(solution)/shard_map/ppermute | solution.py:117
  203.7 5.4 %project.3 = (bf16[256,1536]{1,0:T(8,128)(2,1)S(1)}, bf16[256,1536]{1,0:T(8,128)(2,1)S(1)}, bf16[256,1536]{1,0:T(8,128)(2,1)S(1)}, bf16[256,1536]{1,0:T(8,128)(2,1)S(1)}) custom-call(bf16[256,1024]{1,0:T(8,128)(2,1)S(1)} %copy-done.22, bf16[256,1024]{1,0:T(8,128)(2,1)S(1)} %collective-permute-done.refs_1_.refs_2_, ...), custom_call_target="tpu_custom_call" | custom-call | flops 3221225472 | bytes 11534336 | tf_op jit(solution)/shard_map/project/pallas_call | solution.py:47
  213.4 16.3 %collective-permute-done.15.refs_1_ = bf16[256,1536]{1,0:T(8,128)(2,1)S(1)} collective-permute-done((bf16[256,1536]{1,0:T(8,128)(2,1)S(1)}, bf16[256,1536]{1,0:T(8,128)(2,1)S(1)}, u32[]{:S(2)}, u32[]{:S(2)}) %collective-permute-start.15) | collective-permute-done | bytes 786464 | tf_op jit(solution)/shard_map/ppermute | solution.py:117
  229.7 14.0 %collective-permute-done.16.refs_2_ = bf16[256,1536]{1,0:T(8,128)(2,1)S(1)} collective-permute-done((bf16[256,1536]{1,0:T(8,128)(2,1)S(1)}, bf16[256,1536]{1,0:T(8,128)(2,1)S(1)}, u32[]{:S(2)}, u32[]{:S(2)}) %collective-permute-start.16) | collective-permute-done | bytes 786464 | tf_op jit(solution)/shard_map/ppermute | solution.py:117
  245.6 5.4 %attention.1.refs_0_.refs_8_ = bf16[256,1536]{1,0:T(8,128)(2,1)S(1)} custom-call(s32[1]{0:T(128)S(6)} %copy.10.length_ref, bf16[256,1536]{1,0:T(8,128)(2,1)S(1)} %get-tuple-element.69.refs_0_, bf16[256,1536]{1,0:T(8,128)(2,1)S(1)} %collective-permute-done.15.refs_1_, bf16[256,1536]{1,0:T(8,128)(2,1)S(1)} %collective-permute-done.16.refs_2_, ...), custom_call_target="tpu_custom_call" | custom-call | flops 805306368 | bytes 4456448 | tf_op jit(solution)/shard_map/attention/pallas_call | solution.py:47
  254.6 17.0 %collective-permute-done.19.refs_2_.refs_10_ = bf16[256,1536]{1,0:T(8,128)(2,1)S(1)} collective-permute-done((bf16[256,1536]{1,0:T(8,128)(2,1)S(1)}, bf16[256,1536]{1,0:T(8,128)(2,1)S(1)}, u32[]{:S(2)}, u32[]{:S(2)}) %collective-permute-start.19) | collective-permute-done | bytes 786464 | tf_op jit(solution)/shard_map/ppermute | solution.py:117
  271.6 14.1 %collective-permute-done.21.refs_4_.refs_12_ = bf16[256,1536]{1,0:T(8,128)(2,1)S(1)} collective-permute-done((bf16[256,1536]{1,0:T(8,128)(2,1)S(1)}, bf16[256,1536]{1,0:T(8,128)(2,1)S(1)}, u32[]{:S(2)}, u32[]{:S(2)}) %collective-permute-start.21) | collective-permute-done | bytes 786464 | tf_op jit(solution)/shard_map/ppermute | solution.py:117
  289.1 6.9 %input_terms.1 = bf16[4,8,256,256]{3,2,1,0:T(8,128)(2,1)S(1)} custom-call(bf16[256,1536]{1,0:T(8,128)(2,1)S(1)} %attention.1.refs_0_.refs_8_, bf16[256,1536]{1,0:T(8,128)(2,1)S(1)} %collective-permute-done.18.refs_1_.refs_9_, bf16[256,1536]{1,0:T(8,128)(2,1)S(1)} %collective-permute-done.19.refs_2_.refs_10_, ...), custom_call_target="tpu_custom_call" | custom-call | flops 6442450944 | bytes 13631488 | tf_op jit(solution)/shard_map/input_terms/pallas_call | solution.py:47
  305.3 4.9 all-to-all-start.1
  310.1 2.8 copy-done
  318.4 7.0 %collective-permute-done.40.refs_2_ = bf16[256,768]{1,0:T(8,128)(2,1)S(1)} collective-permute-done((bf16[256,768]{1,0:T(8,128)(2,1)S(1)}, bf16[256,768]{1,0:T(8,128)(2,1)S(1)}, u32[]{:S(2)}, u32[]{:S(2)}) %collective-permute-start.40) | collective-permute-done | bytes 393248 | tf_op jit(solution)/shard_map/ppermute | solution.py:117
  325.5 7.4 %collective-permute-done.41.refs_3_ = bf16[256,768]{1,0:T(8,128)(2,1)S(1)} collective-permute-done((bf16[256,768]{1,0:T(8,128)(2,1)S(1)}, bf16[256,768]{1,0:T(8,128)(2,1)S(1)}, u32[]{:S(2)}, u32[]{:S(2)}) %collective-permute-start.41) | collective-permute-done | bytes 393248 | tf_op jit(solution)/shard_map/ppermute | solution.py:117
  333.0 18.4 %collective-permute-done.43.refs_5_ = bf16[256,768]{1,0:T(8,128)(2,1)S(1)} collective-permute-done((bf16[256,768]{1,0:T(8,128)(2,1)S(1)}, bf16[256,768]{1,0:T(8,128)(2,1)S(1)}, u32[]{:S(2)}, u32[]{:S(2)}) %collective-permute-start.43) | collective-permute-done | bytes 393248 | tf_op jit(solution)/shard_map/ppermute | solution.py:117
  353.3 50.6 %all-to-all-done.1.in_ref = bf16[4,8,256,256]{3,2,1,0:T(8,128)(2,1)} async-done(((bf16[4,8,256,256]{3,2,1,0:T(8,128)(2,1)}), bf16[4,8,256,256]{3,2,1,0:T(8,128)(2,1)}, u32[]{:S(2)}, u32[]{:S(2)}) %all-to-all-start.1) | async-done | bytes 4194336 | tf_op jit(solution)/shard_map/all_to_all | solution.py:125
  403.9 4.7 all-to-all-start.3
  408.6 3.2 sum_terms.1
  418.5 60.5 %all-to-all-done.3 = bf16[8,256,768]{2,1,0:T(8,128)(2,1)} async-done(((bf16[8,256,768]{2,1,0:T(8,128)(2,1)}), bf16[8,256,768]{2,1,0:T(8,128)(2,1)}, u32[]{:S(2)}, u32[]{:S(2)}) %all-to-all-start.3) | async-done | bytes 3145760 | tf_op jit(solution)/shard_map/all_to_all | solution.py:125
  496.5 17.0 %update.1 = (bf16[4,1,256,1536]{3,2,1,0:T(8,128)(2,1)}, f32[4,1,256,1536]{3,2,1,0:T(8,128)}, f32[4,1,256,1536]{3,2,1,0:T(8,128)}) custom-call(bf16[256,1024]{1,0:T(8,128)(2,1)S(1)} %copy-done.23, bf16[256,1024]{1,0:T(8,128)(2,1)S(1)} %copy-done.26, bf16[256,1024]{1,0:T(8,128)(2,1)S(1)} %copy-done.37, bf16[256,1024]{1,0:T(8,128)(2,1)S(1)} %copy-done.29, ...), custom_call_target="tpu_custom_call" | custom-call | flops 6442450944 | bytes 35651584 | tf_op jit(solution)/shard_map/update/pallas_call | solution.py:283
  (177 shorter events, 102.6 us)
Async XLA Ops:
  7.7 34.1 %collective-permute-start.7 = (bf16[256,768]{1,0:T(8,128)(2,1)S(1)}, bf16[256,768]{1,0:T(8,128)(2,1)S(1)}, u32[]{:S(2)}, u32[]{:S(2)}) collective-permute-start(bf16[256,768]{1,0:T(8,128)(2,1)S(1)} %get-tuple-element.62), channel_id=1, source_target_pairs={{0,20},{4,16},{8,28},{12,24},{16,4},{20,0},{24,12},{28,8},{1,21},{... | collective-permute-start | bytes 1179656 | tf_op jit(solution)/shard_map/ppermute | solution.py:117
  7.7 34.1 %collective-permute-start.8 = (bf16[256,768]{1,0:T(8,128)(2,1)S(1)}, bf16[256,768]{1,0:T(8,128)(2,1)S(1)}, u32[]{:S(2)}, u32[]{:S(2)}) collective-permute-start(bf16[256,768]{1,0:T(8,128)(2,1)S(1)} %get-tuple-element.63), channel_id=1, source_target_pairs={{0,24},{4,28},{8,16},{12,20},{16,8},{20,12},{24,0},{28,4},{1,25},{... | collective-permute-start | bytes 1179656 | tf_op jit(solution)/shard_map/ppermute | solution.py:117
  15.8 26.0 %collective-permute-start.9 = (bf16[256,768]{1,0:T(8,128)(2,1)S(1)}, bf16[256,768]{1,0:T(8,128)(2,1)S(1)}, u32[]{:S(2)}, u32[]{:S(2)}) collective-permute-start(bf16[256,768]{1,0:T(8,128)(2,1)S(1)} %get-tuple-element.64), channel_id=1, source_target_pairs={{0,28},{4,24},{8,20},{12,16},{16,12},{20,8},{24,4},{28,0},{1,29},{... | collective-permute-start | bytes 1179656 | tf_op jit(solution)/shard_map/ppermute | solution.py:117
  43.7 76.5 %all-to-all-start = ((bf16[8,256,768]{2,1,0:T(8,128)(2,1)}), bf16[8,256,768]{2,1,0:T(8,128)(2,1)S(1)}, u32[]{:S(2)}, u32[]{:S(2)}) async-start(bf16[8,256,768]{2,1,0:T(8,128)(2,1)} %place_blocks.3), calls=%async_computation | async-start | bytes 6291456 | tf_op jit(solution)/shard_map/all_to_all | solution.py:125
  56.6 25.2 %collective-permute-start.12 = (bf16[256,1024]{1,0:T(8,128)(2,1)S(1)}, bf16[256,1024]{1,0:T(8,128)(2,1)S(1)}, u32[]{:S(2)}, u32[]{:S(2)}) collective-permute-start(bf16[256,1024]{1,0:T(8,128)(2,1)S(1)} %get-tuple-element.67), channel_id=1, source_target_pairs={{0,20},{4,16},{8,28},{12,24},{16,4},{20,0},{24,12},{28,8},{1,21},{... | collective-permute-start | bytes 1572872 | tf_op jit(solution)/shard_map/ppermute | solution.py:117
  57.8 24.8 %collective-permute-start.13 = (bf16[256,1024]{1,0:T(8,128)(2,1)S(1)}, bf16[256,1024]{1,0:T(8,128)(2,1)S(1)}, u32[]{:S(2)}, u32[]{:S(2)}) collective-permute-start(bf16[256,1024]{1,0:T(8,128)(2,1)S(1)} %get-tuple-element.68), channel_id=1, source_target_pairs={{0,28},{4,24},{8,20},{12,16},{16,12},{20,8},{24,4},{28,0},{1,29},{... | collective-permute-start | bytes 1572872 | tf_op jit(solution)/shard_map/ppermute | solution.py:117
  129.8 72.5 %collective-permute-start.14 = (bf16[4,256,1536]{2,1,0:T(8,128)(2,1)}, bf16[4,256,1536]{2,1,0:T(8,128)(2,1)}, u32[]{:S(2)}, u32[]{:S(2)}) collective-permute-start(bf16[4,256,1536]{2,1,0:T(8,128)(2,1)} %project.2), channel_id=1, source_target_pairs={{0,4},{4,0},{8,12},{12,8},{16,20},{20,16},{24,28},{28,24},{1,5},{5... | collective-permute-start | bytes 9437192 | tf_op jit(solution)/shard_map/ppermute | solution.py:117
  132.2 17.9 %collective-permute-start.34 = (bf16[256,768]{1,0:T(8,128)(2,1)S(1)}, bf16[256,768]{1,0:T(8,128)(2,1)S(1)}, u32[]{:S(2)}, u32[]{:S(2)}) collective-permute-start(bf16[256,768]{1,0:T(8,128)(2,1)S(1)} %get-tuple-element.85), channel_id=1, source_target_pairs={{0,12},{4,8},{8,4},{12,0},{16,28},{20,24},{24,20},{28,16},{1,13},{... | collective-permute-start | bytes 1179656 | tf_op jit(solution)/shard_map/ppermute | solution.py:117
  132.2 21.1 %collective-permute-start.35 = (bf16[256,768]{1,0:T(8,128)(2,1)S(1)}, bf16[256,768]{1,0:T(8,128)(2,1)S(1)}, u32[]{:S(2)}, u32[]{:S(2)}) collective-permute-start(bf16[256,768]{1,0:T(8,128)(2,1)S(1)} %get-tuple-element.86), channel_id=1, source_target_pairs={{0,16},{4,20},{8,24},{12,28},{16,0},{20,4},{24,8},{28,12},{1,17},{... | collective-permute-start | bytes 1179656 | tf_op jit(solution)/shard_map/ppermute | solution.py:117
  136.1 32.8 %collective-permute-start.36 = (bf16[256,768]{1,0:T(8,128)(2,1)S(1)}, bf16[256,768]{1,0:T(8,128)(2,1)S(1)}, u32[]{:S(2)}, u32[]{:S(2)}) collective-permute-start(bf16[256,768]{1,0:T(8,128)(2,1)S(1)} %get-tuple-element.87), channel_id=1, source_target_pairs={{0,20},{4,16},{8,28},{12,24},{16,4},{20,0},{24,12},{28,8},{1,21},{... | collective-permute-start | bytes 1179656 | tf_op jit(solution)/shard_map/ppermute | solution.py:117
  142.7 26.2 %collective-permute-start.37 = (bf16[256,768]{1,0:T(8,128)(2,1)S(1)}, bf16[256,768]{1,0:T(8,128)(2,1)S(1)}, u32[]{:S(2)}, u32[]{:S(2)}) collective-permute-start(bf16[256,768]{1,0:T(8,128)(2,1)S(1)} %get-tuple-element.88), channel_id=1, source_target_pairs={{0,24},{4,28},{8,16},{12,20},{16,8},{20,12},{24,0},{28,4},{1,25},{... | collective-permute-start | bytes 1179656 | tf_op jit(solution)/shard_map/ppermute | solution.py:117
  150.1 18.7 %collective-permute-start.38 = (bf16[256,768]{1,0:T(8,128)(2,1)S(1)}, bf16[256,768]{1,0:T(8,128)(2,1)S(1)}, u32[]{:S(2)}, u32[]{:S(2)}) collective-permute-start(bf16[256,768]{1,0:T(8,128)(2,1)S(1)} %get-tuple-element.89), channel_id=1, source_target_pairs={{0,28},{4,24},{8,20},{12,16},{16,12},{20,8},{24,4},{28,0},{1,29},{... | collective-permute-start | bytes 1179656 | tf_op jit(solution)/shard_map/ppermute | solution.py:117
  170.7 134.5 %all-to-all-start.2 = ((bf16[8,256,768]{2,1,0:T(8,128)(2,1)}), bf16[8,256,768]{2,1,0:T(8,128)(2,1)}, u32[]{:S(2)}, u32[]{:S(2)}) async-start(bf16[8,256,768]{2,1,0:T(8,128)(2,1)} %place_blocks.4), calls=%async_computation.2 | async-start | bytes 6291456 | tf_op jit(solution)/shard_map/all_to_all | solution.py:125
  177.2 25.1 %collective-permute-start.1 = (bf16[256,1024]{1,0:T(8,128)(2,1)}, bf16[256,1024]{1,0:T(8,128)(2,1)S(1)}, u32[]{:S(2)}, u32[]{:S(2)}) collective-permute-start(bf16[256,1024]{1,0:T(8,128)(2,1)} %copy-done.43), channel_id=1, source_target_pairs={{0,16},{4,20},{8,24},{12,28},{16,0},{20,4},{24,8},{28,12},{1,17},{... | collective-permute-start | bytes 1572872 | tf_op jit(solution)/shard_map/ppermute | solution.py:117
  178.7 23.6 %collective-permute-start.2 = (bf16[256,1024]{1,0:T(8,128)(2,1)}, bf16[256,1024]{1,0:T(8,128)(2,1)S(1)}, u32[]{:S(2)}, u32[]{:S(2)}) collective-permute-start(bf16[256,1024]{1,0:T(8,128)(2,1)} %copy-done.42), channel_id=1, source_target_pairs={{0,24},{4,28},{8,16},{12,20},{16,8},{20,12},{24,0},{28,4},{1,25},{... | collective-permute-start | bytes 1572872 | tf_op jit(solution)/shard_map/ppermute | solution.py:117
  209.2 20.5 %collective-permute-start.15 = (bf16[256,1536]{1,0:T(8,128)(2,1)S(1)}, bf16[256,1536]{1,0:T(8,128)(2,1)S(1)}, u32[]{:S(2)}, u32[]{:S(2)}) collective-permute-start(bf16[256,1536]{1,0:T(8,128)(2,1)S(1)} %get-tuple-element.70), channel_id=1, source_target_pairs={{0,8},{4,12},{8,0},{12,4},{16,24},{20,28},{24,16},{28,20},{1,9},{5... | collective-permute-start | bytes 2359304 | tf_op jit(solution)/shard_map/ppermute | solution.py:117
  210.3 33.5 %collective-permute-start.16 = (bf16[256,1536]{1,0:T(8,128)(2,1)S(1)}, bf16[256,1536]{1,0:T(8,128)(2,1)S(1)}, u32[]{:S(2)}, u32[]{:S(2)}) collective-permute-start(bf16[256,1536]{1,0:T(8,128)(2,1)S(1)} %get-tuple-element.71), channel_id=1, source_target_pairs={{0,16},{4,20},{8,24},{12,28},{16,0},{20,4},{24,8},{28,12},{1,17},{... | collective-permute-start | bytes 2359304 | tf_op jit(solution)/shard_map/ppermute | solution.py:117
  211.3 34.3 %collective-permute-start.17 = (bf16[256,1536]{1,0:T(8,128)(2,1)S(1)}, bf16[256,1536]{1,0:T(8,128)(2,1)S(1)}, u32[]{:S(2)}, u32[]{:S(2)}) collective-permute-start(bf16[256,1536]{1,0:T(8,128)(2,1)S(1)} %get-tuple-element.72), channel_id=1, source_target_pairs={{0,24},{4,28},{8,16},{12,20},{16,8},{20,12},{24,0},{28,4},{1,25},{... | collective-permute-start | bytes 2359304 | tf_op jit(solution)/shard_map/ppermute | solution.py:117
  251.0 20.5 %collective-permute-start.19 = (bf16[256,1536]{1,0:T(8,128)(2,1)S(1)}, bf16[256,1536]{1,0:T(8,128)(2,1)S(1)}, u32[]{:S(2)}, u32[]{:S(2)}) collective-permute-start(bf16[256,1536]{1,0:T(8,128)(2,1)S(1)} %attention.1.refs_0_.refs_8_), channel_id=1, source_target_pairs={{0,8},{4,12},{8,0},{12,4},{16,24},{20,28},{24,16},{28,20},{1,9},{5... | collective-permute-start | bytes 2359304 | tf_op jit(solution)/shard_map/ppermute | solution.py:117
  251.7 34.0 %collective-permute-start.21 = (bf16[256,1536]{1,0:T(8,128)(2,1)S(1)}, bf16[256,1536]{1,0:T(8,128)(2,1)S(1)}, u32[]{:S(2)}, u32[]{:S(2)}) collective-permute-start(bf16[256,1536]{1,0:T(8,128)(2,1)S(1)} %attention.1.refs_0_.refs_8_), channel_id=1, source_target_pairs={{0,16},{4,20},{8,24},{12,28},{16,0},{20,4},{24,8},{28,12},{1,17},{... | collective-permute-start | bytes 2359304 | tf_op jit(solution)/shard_map/ppermute | solution.py:117
  253.4 32.3 %collective-permute-start.23 = (bf16[256,1536]{1,0:T(8,128)(2,1)S(1)}, bf16[256,1536]{1,0:T(8,128)(2,1)S(1)}, u32[]{:S(2)}, u32[]{:S(2)}) collective-permute-start(bf16[256,1536]{1,0:T(8,128)(2,1)S(1)} %attention.1.refs_0_.refs_8_), channel_id=1, source_target_pairs={{0,24},{4,28},{8,16},{12,20},{16,8},{20,12},{24,0},{28,4},{1,25},{... | collective-permute-start | bytes 2359304 | tf_op jit(solution)/shard_map/ppermute | solution.py:117
  254.6 31.6 %collective-permute-start.18 = (bf16[256,1536]{1,0:T(8,128)(2,1)S(1)}, bf16[256,1536]{1,0:T(8,128)(2,1)S(1)}, u32[]{:S(2)}, u32[]{:S(2)}) collective-permute-start(bf16[256,1536]{1,0:T(8,128)(2,1)S(1)} %attention.1.refs_0_.refs_8_), channel_id=1, source_target_pairs={{0,4},{4,0},{8,12},{12,8},{16,20},{20,16},{24,28},{28,24},{1,5},{5... | collective-permute-start | bytes 2359304 | tf_op jit(solution)/shard_map/ppermute | solution.py:117
  305.3 98.6 %all-to-all-start.1 = ((bf16[4,8,256,256]{3,2,1,0:T(8,128)(2,1)}), bf16[4,8,256,256]{3,2,1,0:T(8,128)(2,1)}, u32[]{:S(2)}, u32[]{:S(2)}) async-start(bf16[4,8,256,256]{3,2,1,0:T(8,128)(2,1)} %copy-done.2), calls=%async_computation.1 | async-start | bytes 8388608 | tf_op jit(solution)/shard_map/all_to_all | solution.py:125
  316.8 34.6 %collective-permute-start.43 = (bf16[256,768]{1,0:T(8,128)(2,1)S(1)}, bf16[256,768]{1,0:T(8,128)(2,1)S(1)}, u32[]{:S(2)}, u32[]{:S(2)}) collective-permute-start(bf16[256,768]{1,0:T(8,128)(2,1)S(1)} %get-tuple-element.96), channel_id=1, source_target_pairs={{0,20},{4,16},{8,28},{12,24},{16,4},{20,0},{24,12},{28,8},{1,21},{... | collective-permute-start | bytes 1179656 | tf_op jit(solution)/shard_map/ppermute | solution.py:117
  316.9 34.5 %collective-permute-start.44 = (bf16[256,768]{1,0:T(8,128)(2,1)S(1)}, bf16[256,768]{1,0:T(8,128)(2,1)S(1)}, u32[]{:S(2)}, u32[]{:S(2)}) collective-permute-start(bf16[256,768]{1,0:T(8,128)(2,1)S(1)} %get-tuple-element.97), channel_id=1, source_target_pairs={{0,24},{4,28},{8,16},{12,20},{16,8},{20,12},{24,0},{28,4},{1,25},{... | collective-permute-start | bytes 1179656 | tf_op jit(solution)/shard_map/ppermute | solution.py:117
  325.4 26.0 %collective-permute-start.45 = (bf16[256,768]{1,0:T(8,128)(2,1)S(1)}, bf16[256,768]{1,0:T(8,128)(2,1)S(1)}, u32[]{:S(2)}, u32[]{:S(2)}) collective-permute-start(bf16[256,768]{1,0:T(8,128)(2,1)S(1)} %get-tuple-element.98), channel_id=1, source_target_pairs={{0,28},{4,24},{8,20},{12,16},{16,12},{20,8},{24,4},{28,0},{1,29},{... | collective-permute-start | bytes 1179656 | tf_op jit(solution)/shard_map/ppermute | solution.py:117
  403.9 75.2 %all-to-all-start.3 = ((bf16[8,256,768]{2,1,0:T(8,128)(2,1)}), bf16[8,256,768]{2,1,0:T(8,128)(2,1)}, u32[]{:S(2)}, u32[]{:S(2)}) async-start(bf16[8,256,768]{2,1,0:T(8,128)(2,1)} %place_blocks.5), calls=%async_computation.3 | async-start | bytes 6291456 | tf_op jit(solution)/shard_map/all_to_all | solution.py:125
  413.4 100.1 %collective-permute-start.27 = (bf16[256,256]{1,0:T(8,128)(2,1)}, bf16[256,256]{1,0:T(8,128)(2,1)}, u32[]{:S(2)}, u32[]{:S(2)}) collective-permute-start(bf16[256,256]{1,0:T(8,128)(2,1)} %get-tuple-element.76), channel_id=1, source_target_pairs={{0,12},{4,8},{8,4},{12,0},{16,28},{20,24},{24,20},{28,16},{1,13},{... | collective-permute-start | bytes 393224 | tf_op jit(solution)/shard_map/ppermute | solution.py:117
  413.6 99.9 %collective-permute-start.28 = (bf16[256,256]{1,0:T(8,128)(2,1)}, bf16[256,256]{1,0:T(8,128)(2,1)}, u32[]{:S(2)}, u32[]{:S(2)}) collective-permute-start(bf16[256,256]{1,0:T(8,128)(2,1)} %get-tuple-element.77), channel_id=1, source_target_pairs={{0,16},{4,20},{8,24},{12,28},{16,0},{20,4},{24,8},{28,12},{1,17},{... | collective-permute-start | bytes 393224 | tf_op jit(solution)/shard_map/ppermute | solution.py:117
  415.3 98.2 %collective-permute-start.29 = (bf16[256,256]{1,0:T(8,128)(2,1)}, bf16[256,256]{1,0:T(8,128)(2,1)}, u32[]{:S(2)}, u32[]{:S(2)}) collective-permute-start(bf16[256,256]{1,0:T(8,128)(2,1)} %get-tuple-element.78), channel_id=1, source_target_pairs={{0,20},{4,16},{8,28},{12,24},{16,4},{20,0},{24,12},{28,8},{1,21},{... | collective-permute-start | bytes 393224 | tf_op jit(solution)/shard_map/ppermute | solution.py:117
  415.3 98.2 %collective-permute-start.30 = (bf16[256,256]{1,0:T(8,128)(2,1)}, bf16[256,256]{1,0:T(8,128)(2,1)}, u32[]{:S(2)}, u32[]{:S(2)}) collective-permute-start(bf16[256,256]{1,0:T(8,128)(2,1)} %get-tuple-element.79), channel_id=1, source_target_pairs={{0,24},{4,28},{8,16},{12,20},{16,8},{20,12},{24,0},{28,4},{1,25},{... | collective-permute-start | bytes 393224 | tf_op jit(solution)/shard_map/ppermute | solution.py:117
  418.0 95.5 %collective-permute-start.31 = (bf16[256,256]{1,0:T(8,128)(2,1)}, bf16[256,256]{1,0:T(8,128)(2,1)}, u32[]{:S(2)}, u32[]{:S(2)}) collective-permute-start(bf16[256,256]{1,0:T(8,128)(2,1)} %get-tuple-element.80), channel_id=1, source_target_pairs={{0,28},{4,24},{8,20},{12,16},{16,12},{20,8},{24,4},{28,0},{1,29},{... | collective-permute-start | bytes 393224 | tf_op jit(solution)/shard_map/ppermute | solution.py:117
  (65 other events, 319.5 us)

commit v2 on v1

v2 whole, which is shorter than its diff:
```python
import functools

import jax
import jax.numpy as jnp
from jax import lax
from jax.experimental import pallas as pl
from jax.experimental.pallas import tpu as pltpu
from jax.sharding import PartitionSpec as P

QUERY_HEADS = 32
KEY_VALUE_HEADS = 8
HEAD_SIZE = 128


beta_first = 0.9
beta_second = 0.95
adam_eps = 1e-08
learn_rate = 0.002
decay_rate = 0.1
bias_first = 1.0 - beta_first**20
bias_second = 1.0 - beta_second**20

MIB = 1 << 20
MICROSECOND = 10**9
SMEM = pl.BlockSpec(memory_space=pltpu.SMEM)


def adam_update(param, gradient, first, second):
    first_new = beta_first * first + (1.0 - beta_first) * gradient
    second_new = beta_second * second + (1.0 - beta_second) * gradient * gradient
    ratio = first_new / bias_first / (jnp.sqrt(second_new / bias_second) + adam_eps)
    widened = param.astype(jnp.float32)
    updated = (widened - learn_rate * (ratio + decay_rate * widened)).astype(jnp.bfloat16)
    return (updated, first_new, second_new)


def shape_of(dims, dtype=jnp.bfloat16):
    return jax.ShapeDtypeStruct(dims, dtype)


def size_of(arrays):
    return sum(a.size * a.dtype.itemsize for a in arrays)


def whole_block(operand):
    if isinstance(operand, tuple):
        dims, at = operand[0].shape[1:], operand[1]
        return pl.BlockSpec((None,) + tuple(dims), lambda i: (at,) + (0,) * len(dims))
    dims = operand.shape
    return pl.BlockSpec(tuple(dims), lambda i: (0,) * len(dims))


def array_of(operand):
    return operand[0] if isinstance(operand, tuple) else operand


def whole_call(body, outs, ins, name, flops=0, scalars=1, waits=()):
    arrays = [array_of(x) for x in ins]
    moved = size_of(arrays[scalars:]) + size_of(outs)
    count = len(ins)

    def without(*refs):
        body(*refs[:count], *refs[count + len(waits) :])

    call = pl.pallas_call(
        without,
        grid=(1,),
        out_shape=outs,
        in_specs=[SMEM] * scalars
        + [whole_block(x) for x in ins[scalars:]]
        + [pl.BlockSpec(memory_space=pl.ANY)] * len(waits),
        out_specs=[whole_block(x) for x in outs],
        compiler_params=pltpu.CompilerParams(vmem_limit_bytes=60 * MIB),
        cost_estimate=pl.CostEstimate(flops=0, bytes_accessed=0, transcendentals=0),
        name=name,
    )
    return list(call(*arrays, *waits))


def pack_blocks(me, blocks, first=0, last=None):
    count, rows, columns = blocks.shape
    last = rows if last is None else last

    def body(me_ref, in_ref, *out_refs):
        for k in range(count):
            out_refs[k // 2][k % 2] = in_ref[me_ref[0] ^ k, first:last].astype(jnp.bfloat16)

    return whole_call(body, [shape_of((2, last - first, columns))] * (count // 2), [me, blocks], "pack_blocks")


def merge_rows(low, high):
    tensor_count, parts, rows, columns = low.shape

    def body(low_ref, high_ref, out_ref):
        out_ref[:, :, :rows] = low_ref[...]
        out_ref[:, :, rows:] = high_ref[...]

    outs = [shape_of((tensor_count, parts, rows + high.shape[2], columns))]
    return whole_call(body, outs, [low, high], "merge_rows", scalars=0)[0]


def gate(pieces, waits, cost=0):
    count = len(pieces)
    anywhere = pl.BlockSpec(memory_space=pl.ANY)
    return list(pl.pallas_call(
        lambda *refs: None,
        out_shape=[shape_of(x.shape, x.dtype) for x in pieces],
        in_specs=[anywhere] * (count + len(waits)),
        out_specs=[anywhere] * count,
        input_output_aliases={i: i for i in range(count)},
        cost_estimate=pl.CostEstimate(flops=cost * MICROSECOND, bytes_accessed=0, transcendentals=0),
        name="gate",
    )(*pieces, *waits))


def place_blocks(me, pieces, waits=()):
    count = len(pieces)
    dims = array_of(pieces[0]).shape[-2:]

    def body(me_ref, *refs):
        for k in range(count):
            refs[count][me_ref[0] ^ k] = refs[k][...]

    return whole_call(body, [shape_of((count,) + dims)], [me, *pieces], "place_blocks", waits=waits)[0]


def pack_columns(me, tokens, tensor_count, replica_count, waits=()):
    length, width = tokens.shape
    rows = width // (tensor_count * replica_count)
    chips = replica_count // 2
    dims = (2, length, tensor_count * rows)
    if rows % 128:
        parts = tokens.reshape(length, tensor_count, replica_count, rows).transpose(2, 0, 1, 3)
        pieces = [lax.dynamic_index_in_dim(parts, me[0] ^ k, 0, False) for k in range(replica_count)]
        return [jnp.stack(pieces[2 * m : 2 * m + 2]).reshape(dims) for m in range(chips)]

    def body(me_ref, in_ref, *out_refs):
        for k in range(replica_count):
            for t in range(tensor_count):
                start = pl.multiple_of((t * replica_count + (me_ref[0] ^ k)) * rows, rows)
                out_refs[k // 2][k % 2, :, t * rows : (t + 1) * rows] = in_ref[:, pl.ds(start, rows)]

    return whole_call(body, [shape_of(dims)] * chips, [me, tokens], "pack_columns", waits=waits)


def place_columns(me, pieces, waits=()):
    count = len(pieces)
    length, rows = array_of(pieces[0]).shape[-2:]
    if rows % 128:
        stacked = place_blocks(me, pieces)
        return stacked.transpose(1, 0, 2).reshape(length, count * rows)

    def body(me_ref, *refs):
        for k in range(count):
            start = pl.multiple_of((me_ref[0] ^ k) * rows, rows)
            refs[count][:, pl.ds(start, rows)] = refs[k][...]

    return whole_call(body, [shape_of((length, count * rows))], [me, *pieces], "place_columns", waits=waits)[0]


def swap(x, k):
    if k == 0:
        return x
    return lax.ppermute(x, "dp", [(i, i ^ k) for i in range(lax.axis_size("dp"))])


def swap_tensor(x, j):
    return lax.ppermute(x, "tensor", [(i, i ^ j) for i in range(lax.axis_size("tensor"))])


def to_chips(pairs):
    return [swap(x, 2 * m) for m, x in enumerate(pairs)]


def to_cores(pairs):
    return [view for x in pairs for view in ((x, 0), (swap(x, 1), 1))]


def exchange(pieces):
    return [swap(piece, k) for k, piece in enumerate(pieces)]


def over_tensor(x):
    return lax.all_to_all(x, "tensor", split_axis=0, concat_axis=0, tiled=True)


def project(pairs, weights):
    _, rows, depth = pairs[0].shape
    parts, columns = weights[0].shape[1], weights[0].shape[3]
    count = len(pairs)

    def body(*refs):
        for e in range(parts):
            blocks = [refs[count + at][:, e].reshape(depth, columns) for at in range(2)]
            for k in range(count):
                value = jnp.dot(refs[k][0], blocks[0], preferred_element_type=jnp.float32)
                value = value + jnp.dot(refs[k][1], blocks[1], preferred_element_type=jnp.float32)
                refs[count + 2 + k][:, e * columns : (e + 1) * columns] = value.astype(jnp.bfloat16)

    return whole_call(body, [shape_of((rows, parts * columns))] * count, [*pairs, *weights], "project", scalars=0)


def attention(length, terms, upstream, waits=()):
    count = len(terms)
    rows, columns = terms[0].shape
    query_columns = upstream.shape[1]
    key_value_columns = (columns - query_columns) // 2
    heads = key_value_columns // HEAD_SIZE
    group = QUERY_HEADS // KEY_VALUE_HEADS
    scale = HEAD_SIZE ** (-0.5)

    def body(length_ref, *refs):
        upstream_ref, out_refs = refs[count], refs[count + 1 :]

        def projected(start):
            cut = slice(start, start + HEAD_SIZE)
            total = refs[0][:, cut].astype(jnp.float32)
            for term in refs[1:count]:
                total = total + term[:, cut].astype(jnp.float32)
            return total.astype(jnp.bfloat16)

        def dot(a, b, on_a, on_b):
            return lax.dot_general(a, b, (((on_a,), (on_b,)), ((), ())), preferred_element_type=jnp.float32)

        def store(start, value):
            for out_ref in out_refs:
                out_ref[:, start : start + HEAD_SIZE] = value.astype(jnp.bfloat16)

        live = length_ref[0]
        at = lax.broadcasted_iota(jnp.int32, (rows, rows), 0)
        of = lax.broadcasted_iota(jnp.int32, (rows, rows), 1)
        allowed = (of <= at) & (of < live)
        active = lax.broadcasted_iota(jnp.int32, (rows, HEAD_SIZE), 0) < live
        for g in range(heads):
            key_start = query_columns + g * HEAD_SIZE
            value_start = query_columns + key_value_columns + g * HEAD_SIZE
            key, value = projected(key_start), projected(value_start)
            key_gradient = jnp.zeros((rows, HEAD_SIZE), jnp.float32)
            value_gradient = jnp.zeros((rows, HEAD_SIZE), jnp.float32)
            for n in range(group):
                start = (g * group + n) * HEAD_SIZE
                query = projected(start)
                given = upstream_ref[:, start : start + HEAD_SIZE]
                given = jnp.where(active, given, jnp.zeros_like(given))
                scores = jnp.where(allowed, dot(query, key, 1, 1) * scale, -jnp.inf)
                expo = jnp.exp(scores - jnp.max(scores, -1, keepdims=True))
                probs = expo / jnp.sum(expo, -1, keepdims=True)
                low = probs.astype(jnp.bfloat16)
                attended = dot(low, value, 1, 0)
                delta = jnp.sum(given.astype(jnp.float32) * attended, -1, keepdims=True)
                score_gradient = (probs * (dot(given, value, 1, 1) - delta) * scale).astype(jnp.bfloat16)
                store(start, dot(score_gradient, key, 1, 0))
                key_gradient = key_gradient + dot(score_gradient, query, 0, 0)
                value_gradient = value_gradient + dot(low, given, 0, 0)
            store(key_start, key_gradient)
            store(value_start, value_gradient)

    flops = 2 * heads * group * 6 * rows * rows * HEAD_SIZE
    return whole_call(body, [shape_of((rows, columns))] * 2, [length, *terms, upstream], "attention", flops, waits=waits)


def halving_order(count):
    if count == 1:
        return [0]
    half = [2 * j for j in halving_order(count // 2)]
    return half + [j + 1 for j in half]


def input_terms(place, columns, weights):
    tensor_count, parts, width, cut_columns = weights[0].shape
    count = len(columns)
    rows = columns[0].shape[0]
    half = tensor_count // 2
    order = halving_order(tensor_count)

    def body(place_ref, *refs):
        for at, j in enumerate(order):
            for core in range(2):
                blocks = [refs[count + core][place_ref[0] ^ j, e] for e in range(parts)]
                for k in range(count):
                    total = None
                    for e in range(parts):
                        term = lax.dot_general(
                            refs[k][:, e * cut_columns : (e + 1) * cut_columns],
                            blocks[e],
                            (((1,), (1,)), ((), ())),
                            preferred_element_type=jnp.float32,
                        )
                        total = term if total is None else total + term
                    refs[count + 2 + at // half][at % half, 2 * k + core] = total.astype(jnp.bfloat16)

    outs = [shape_of((half, 2 * count, rows, width))] * 2
    return whole_call(body, outs, [place, *columns, *weights], "input_terms")


def fold_terms(kept, received):
    half = kept.shape[0] // 2
    dims = (half,) + kept.shape[1:]

    def body(kept_ref, received_ref, stay_ref, go_ref):
        for at in range(2 * half):
            total = kept_ref[at].astype(jnp.float32) + received_ref[at].astype(jnp.float32)
            if at < half:
                stay_ref[at] = total
            else:
                go_ref[at - half] = total.astype(jnp.bfloat16)

    outs = [shape_of(dims, jnp.float32), shape_of(dims)]
    return whole_call(body, outs, [kept, received], "fold_terms", scalars=0)


def sum_terms(kept, received, waits=()):
    count = kept.shape[1] // 2

    def body(kept_ref, received_ref, *out_refs):
        for k in range(2 * count):
            total = kept_ref[0, k].astype(jnp.float32) + received_ref[0, k].astype(jnp.float32)
            out_refs[k // 2][k % 2] = total.astype(jnp.bfloat16)

    outs = [shape_of((2,) + kept.shape[2:])] * count
    return whole_call(body, outs, [kept, received], "sum_terms", scalars=0, waits=waits)


def update(pieces, columns, weight, first, second, begin, end, earlier=(), waits=()):
    tensor_count, parts, width, cut_columns = weight.shape
    count = len(pieces)
    rows = columns[0].shape[0]
    dims = (tensor_count, 1, width, parts * cut_columns)
    if width % 128:
        if earlier:
            return earlier
        inputs = jnp.concatenate([x[at] for x, at in pieces], 0)
        gradient = lax.dot_general(
            inputs, jnp.concatenate(columns, 0), (((0,), (0,)), ((), ())), preferred_element_type=jnp.float32
        ).reshape(dims)
        merged = [a.transpose(0, 2, 1, 3).reshape(dims) for a in (weight, first, second)]
        return adam_update(merged[0], gradient, merged[1].astype(jnp.float32), merged[2].astype(jnp.float32))

    def body(*refs):
        weight_ref, first_ref, second_ref = refs[2 * count : 2 * count + 3]
        new_weight, new_first, new_second = refs[-3:]
        gradient = None
        cut = pl.ds(pl.multiple_of(pl.program_id(1) * cut_columns, cut_columns), cut_columns)
        for k in range(count):
            term = lax.dot_general(
                refs[k][...], refs[count + k][:, cut], (((0,), (0,)), ((), ())), preferred_element_type=jnp.float32
            )
            gradient = term if gradient is None else gradient + term
        updated, moved_first, moved_second = adam_update(
            weight_ref[0, 0],
            gradient,
            first_ref[0, 0].astype(jnp.float32),
            second_ref[0, 0].astype(jnp.float32),
        )
        new_weight[0, 0] = updated
        new_first[0, 0] = moved_first
        new_second[0, 0] = moved_second

    old = pl.BlockSpec((1, 1, width, cut_columns), lambda t, e: (begin + t, e, 0, 0))
    new = pl.BlockSpec((1, 1, width, cut_columns), lambda t, e: (begin + t, 0, 0, e))
    outs = [shape_of(dims), shape_of(dims, jnp.float32), shape_of(dims, jnp.float32)]
    ins = [*map(array_of, pieces), *columns, weight, first, second, *earlier, *waits]
    given = len(ins) - len(earlier) - len(waits)
    call = pl.pallas_call(
        body,
        grid=(end - begin, parts),
        out_shape=outs,
        in_specs=[pl.BlockSpec((None, rows, width), lambda t, e, at=at: (at, 0, begin + t)) for _, at in pieces]
        + [pl.BlockSpec((rows, parts * cut_columns), lambda t, e: (0, 0))] * count
        + [old] * 3
        + [pl.BlockSpec(memory_space=pl.ANY)] * (len(earlier) + len(waits)),
        out_specs=[new] * 3,
        input_output_aliases={given + i: i for i in range(len(earlier))},
        compiler_params=pltpu.CompilerParams(vmem_limit_bytes=60 * MIB),
        cost_estimate=pl.CostEstimate(flops=0, bytes_accessed=0, transcendentals=0),
        name="update",
    )
    return list(call(*ins))


def local(tokens, grad_out, lengths, weights, moment1, moment2):
    tensor_count = lax.axis_size("tensor")
    replica_count = lax.axis_size("dp")
    width, cut_columns = weights.shape[2:]
    parts = replica_count // tensor_count
    me = lax.axis_index("dp").astype(jnp.int32).reshape(1)
    place = lax.axis_index("tensor").astype(jnp.int32).reshape(1)
    new_split = (tensor_count, parts, width, cut_columns)

    chips = replica_count // 2

    def next_transfer(received, following, meanwhile=(), cost=0):
        held = gate(received[1:] + following, meanwhile, cost)
        return received[:1] + held[: chips - 1], held[chips - 1 :]

    cut = max(width * 6 // 16 // 16, 1) * 16
    packed_low, packed_high = pack_blocks(me, weights[0], 0, cut), pack_blocks(me, weights[0], cut)
    packed_first = pack_blocks(me, moment1[0])
    packed_second = pack_blocks(me, moment2[0])
    received, packed_high = next_transfer(to_chips(packed_low), packed_high, packed_first[:1], 8)
    low_rows = place_blocks(me, to_cores(received))
    packed_tokens = pack_columns(me, tokens, tensor_count, replica_count, (low_rows,))
    received, packed_first = next_transfer(
        to_chips(packed_high), packed_first, [packed_tokens[0]], 15
    )
    high_rows = place_blocks(me, to_cores(received))
    weight = merge_rows(
        *(over_tensor(x).reshape(tensor_count, parts, x.shape[1], cut_columns) for x in (low_rows, high_rows))
    )
    received, packed_tokens = next_transfer(to_chips(packed_first), packed_tokens, [high_rows, packed_second[0]], 15)
    first_rows = place_blocks(me, to_cores(received))
    first = over_tensor(first_rows).reshape(new_split)
    token_pairs, packed_second = next_transfer(
        to_chips(packed_tokens), packed_second + [weight], [first_rows], 0
    )
    weight = packed_second.pop()
    weights_pair = [weight, swap(weight, 1)]

    sums = project(token_pairs, weights_pair)
    received, sums = next_transfer(to_chips(packed_second), sums, (), 0)
    second_rows = place_blocks(me, to_cores(received))
    second = over_tensor(second_rows).reshape(new_split)
    terms, _ = next_transfer(to_chips(sums), [], [second_rows], 15)
    columns, columns_again = attention(lengths, terms, grad_out)

    def begin(columns):
        kept, sent = input_terms(place, columns, weights_pair)
        return kept, swap_tensor(sent, 1)

    def proceed(kept, received):
        step = 2
        while step < tensor_count:
            kept, sent = fold_terms(kept, received)
            received = swap_tensor(sent, step)
            step *= 2
        return kept, received

    near = [swap(columns, 2 * m) for m in range(1, chips - 1)]
    far = swap(gate([columns_again], near)[0] if 1 else columns, 2 * (chips - 1))
    own_state = begin([columns])
    near = gate(near, own_state[:1], 8)
    near_state = begin(near)
    if 0:
        own_state = proceed(*own_state)
    (far,) = gate([far], [own_state[0], near_state[0]], 8)
    far_state = begin([far])
    same_core = [columns, *near, far]
    all_columns = [x for pair in zip(same_core, [swap(x, 1) for x in same_core]) for x in pair]
    operands = (to_cores(token_pairs), all_columns, weight, first, second)
    some = update(*operands, 0, tensor_count // 2)
    own_state = proceed(*own_state)
    near_state = proceed(near_state[0], gate(near_state[1:], some[:1])[0])
    far_state = proceed(*far_state)
    near_sums = sum_terms(*near_state)
    new_weights, new_first, new_second = update(*operands, tensor_count // 2, tensor_count, some, near_sums[:1])
    near_sums = [swap(x, 2 * m + 2) for m, x in enumerate(near_sums)]
    (far_sum,) = sum_terms(far_state[0], gate(far_state[1:], [new_weights, *near_sums])[0])
    pairs = [*sum_terms(*own_state), *near_sums, swap(far_sum, 2 * (chips - 1))]
    input_grad = place_columns(me, [(x, at) for x in pairs for at in range(2)], (new_weights,))
    return (input_grad, new_weights, new_first, new_second)


def solution(mesh):
    return jax.shard_map(
        local,
        mesh=mesh,
        in_specs=(
            P("dp", None),
            P("dp", "tensor"),
            P("dp"),
            P("tensor", None, None, "dp"),
            P("tensor", None, None, "dp"),
            P("tensor", None, None, "dp"),
        ),
        out_specs=(
            P("dp", "tensor"),
            P(None, "dp", None, "tensor"),
            P(None, "dp", None, "tensor"),
            P(None, "dp", None, "tensor"),
        ),
        check_vma=False,
    )
```

time: 517 us -> 354 us (0.68)
  waiting for transfers between devices: 351 us -> 164 us
  Pallas kernels: 52.4 us -> 116 us
  local copies, waits for them, and re-layouts: 45.8 us -> 13.1 us
  starting transfers between devices: 64.7 us -> 58.3 us
    all_to_all x4, waiting for transfers between devices: 148 us -> 25.5 us  [over_tensor(): return lax.all_to_all(x, 'tensor', split_axis=0, concat_axis=0, tiled=True)]
    ppermute x46 -> x49, waiting for transfers between devices: 203 us -> 113 us  [swap(): lax.ppermute(x, 'dp', [(i, i ^ k) for i in range(lax.axis_size('dp'))])]
    pallas_call x14 -> x35, Pallas kernels: 52.4 us -> 116 us  [the longest x22 92 us: whole_call(): return list(call(*arrays, *waits))]
    unnamed x94 -> x64, local copies, waits for them, and re-layouts: 45.8 us -> 13.1 us
    ppermute x0 -> x6, waiting for transfers between devices: none -> 26.3 us  [swap_tensor(): lax.ppermute(x, 'tensor', [(i, i ^ j) for i in range(lax.axis_size('tenso...]
    ppermute x46 -> x49, starting transfers between devices: 45 us -> 34.3 us  [swap(): lax.ppermute(x, 'dp', [(i, i ^ k) for i in range(lax.axis_size('dp'))])]
    ppermute x0 -> x6, starting transfers between devices: none -> 6.19 us  [swap_tensor(): lax.ppermute(x, 'tensor', [(i, i ^ j) for i in range(lax.axis_size('tenso...]
  transfers between devices with their start and end apart: 50 -> 59, of which waited for: 25 -> 28; matrix products, arithmetic and copies ran while one was open for 0% -> 0% of each run, Pallas kernels for 8% -> 31%
where the time goes in v2:
time: 354 us; the launch traced here: 353 us
  waiting for transfers between devices  164 us (46%)
  Pallas kernels  116 us (33%)
  starting transfers between devices  58.3 us (16%)
  local copies, waits for them, and re-layouts  13.1 us (4%)
    ppermute x49, waiting for transfers between devices, swap(): lax.ppermute(x, 'dp', [(i, i ^ k) for i in range(lax.axis_size('dp'))])  113 us
    pallas_call x22, Pallas kernels, whole_call(): return list(call(*arrays, *waits))  92 us
    ppermute x49, starting transfers between devices, swap(): lax.ppermute(x, 'dp', [(i, i ^ k) for i in range(lax.axis_size('dp'))])  34.3 us
    ppermute x6, waiting for transfers between devices, swap_tensor(): lax.ppermute(x, 'tensor', [(i, i ^ j) for i in range(lax.axis_size('tenso...  26.3 us
    all_to_all x4, waiting for transfers between devices, over_tensor(): return lax.all_to_all(x, 'tensor', split_axis=0, concat_axis=0, tiled=True)  25.5 us
    pallas_call x2, Pallas kernels, update(): return list(call(*ins))  24.1 us
    all_to_all x4, starting transfers between devices, over_tensor(): return lax.all_to_all(x, 'tensor', split_axis=0, concat_axis=0, tiled=True)  17.8 us
    unnamed x64, local copies, waits for them, and re-layouts  13.1 us
  transfers between devices with their start and end apart: 59, of which 28 were waited for; matrix products, arithmetic and copies ran while one was open for 0% of the time, Pallas kernels for 31%

profile of v2, /device:TPU:0, one launch (start us, length us, event | category | flops | bytes accessed | tf_op | source)
XLA Modules:
  0.0 353.4 jit_solution(13143463349444324849)
XLA Ops:
  11.3 4.7 %pack_blocks.6 = (bf16[2,256,768]{2,1,0:T(8,128)(2,1)}, bf16[2,256,768]{2,1,0:T(8,128)(2,1)}, bf16[2,256,768]{2,1,0:T(8,128)(2,1)}, bf16[2,256,768]{2,1,0:T(8,128)(2,1)}) custom-call(s32[1]{0:T(128)} %bitcast.refs_0_, f32[8,256,768]{2,1,0:T(8,128)} %bitcast.13), custom_call_target="tpu_custom_call" | custom-call | tf_op jit(solution)/shard_map/pack_blocks/pallas_call | solution.py:77
  16.1 5.4 %collective-permute-done.1.refs_1_ = bf16[2,96,768]{2,1,0:T(8,128)(2,1)S(1)} collective-permute-done((bf16[2,96,768]{2,1,0:T(8,128)(2,1)}, bf16[2,96,768]{2,1,0:T(8,128)(2,1)S(1)}, u32[]{:S(2)}, u32[]{:S(2)}) %collective-permute-start.1) | collective-permute-done | bytes 294944 | tf_op jit(solution)/shard_map/ppermute | solution.py:164
  31.5 4.9 %all-to-all-start = ((bf16[8,96,768]{2,1,0:T(8,128)(2,1)}), bf16[8,96,768]{2,1,0:T(8,128)(2,1)S(1)}, u32[]{:S(2)}, u32[]{:S(2)}) async-start(bf16[8,96,768]{2,1,0:T(8,128)(2,1)} %place_blocks.4.refs_2_), calls=%async_computation | async-start | bytes 2359296 | tf_op jit(solution)/shard_map/all_to_all | solution.py:184
  36.4 4.9 %pack_columns.1 = (bf16[2,256,1024]{2,1,0:T(8,128)(2,1)}, bf16[2,256,1024]{2,1,0:T(8,128)(2,1)}, bf16[2,256,1024]{2,1,0:T(8,128)(2,1)}, bf16[2,256,1024]{2,1,0:T(8,128)(2,1)}) custom-call(s32[1]{0:T(128)} %bitcast.refs_0_, bf16[256,8192]{1,0:T(8,128)(2,1)} %refs_1_.1, bf16[8,96,768]{2,1,0:T(8,128)(2,1)} %place_blocks.4.refs_2_), custom_call_target="tpu_custom_call" | custom-call | tf_op jit(solution)/shard_map/pack_columns/pallas_call | solution.py:77
  41.3 4.9 %collective-permute-done.4.refs_1_ = bf16[2,160,768]{2,1,0:T(8,128)(2,1)S(1)} collective-permute-done((bf16[2,160,768]{2,1,0:T(8,128)(2,1)}, bf16[2,160,768]{2,1,0:T(8,128)(2,1)S(1)}, u32[]{:S(2)}, u32[]{:S(2)}) %collective-permute-start.4) | collective-permute-done | bytes 491552 | tf_op jit(solution)/shard_map/ppermute | solution.py:164
  52.5 4.7 %pack_blocks.7 = (bf16[2,256,768]{2,1,0:T(8,128)(2,1)}, bf16[2,256,768]{2,1,0:T(8,128)(2,1)}, bf16[2,256,768]{2,1,0:T(8,128)(2,1)}, bf16[2,256,768]{2,1,0:T(8,128)(2,1)}) custom-call(s32[1]{0:T(128)} %bitcast.refs_0_, f32[8,256,768]{2,1,0:T(8,128)} %bitcast.14), custom_call_target="tpu_custom_call" | custom-call | tf_op jit(solution)/shard_map/pack_blocks/pallas_call | solution.py:77
  60.4 4.8 %all-to-all-done = bf16[8,96,768]{2,1,0:T(8,128)(2,1)S(1)} async-done(((bf16[8,96,768]{2,1,0:T(8,128)(2,1)}), bf16[8,96,768]{2,1,0:T(8,128)(2,1)S(1)}, u32[]{:S(2)}, u32[]{:S(2)}) %all-to-all-start) | async-done | bytes 1179680 | tf_op jit(solution)/shard_map/all_to_all | solution.py:184
  65.3 4.4 %all-to-all-start.1 = ((bf16[8,160,768]{2,1,0:T(8,128)(2,1)}), bf16[8,160,768]{2,1,0:T(8,128)(2,1)}, u32[]{:S(2)}, u32[]{:S(2)}) async-start(bf16[8,160,768]{2,1,0:T(8,128)(2,1)} %place_blocks.5.refs_7_), calls=%async_computation.1 | async-start | bytes 3932160 | tf_op jit(solution)/shard_map/all_to_all | solution.py:184
  69.7 16.5 %collective-permute-done.11.refs_1_ = bf16[2,256,768]{2,1,0:T(8,128)(2,1)S(1)} collective-permute-done((bf16[2,256,768]{2,1,0:T(8,128)(2,1)}, bf16[2,256,768]{2,1,0:T(8,128)(2,1)S(1)}, u32[]{:S(2)}, u32[]{:S(2)}) %collective-permute-start.11) | collective-permute-done | bytes 786464 | tf_op jit(solution)/shard_map/ppermute | solution.py:164
  94.7 3.7 %place_blocks.6.refs_8_ = bf16[8,256,768]{2,1,0:T(8,128)(2,1)} custom-call(s32[1]{0:T(128)} %bitcast.refs_0_, bf16[2,256,768]{2,1,0:T(8,128)(2,1)} %get-tuple-element.127.refs_1_, bf16[2,256,768]{2,1,0:T(8,128)(2,1)} %collective-permute-done.20.refs_2_, bf16[2,256,768]{2,1,0:T(8,128)(2,1)} %get-tuple-element.128.refs_3_, ...), custom_call_target="tpu_custom_call" | custom-call | tf_op jit(solution)/shard_map/place_blocks/pallas_call | solution.py:77
  98.3 16.3 %all-to-all-done.1 = bf16[8,160,768]{2,1,0:T(8,128)(2,1)} async-done(((bf16[8,160,768]{2,1,0:T(8,128)(2,1)}), bf16[8,160,768]{2,1,0:T(8,128)(2,1)}, u32[]{:S(2)}, u32[]{:S(2)}) %all-to-all-start.1) | async-done | bytes 1966112 | tf_op jit(solution)/shard_map/all_to_all | solution.py:184
  114.7 4.6 %all-to-all-start.2 = ((bf16[8,256,768]{2,1,0:T(8,128)(2,1)}), bf16[8,256,768]{2,1,0:T(8,128)(2,1)}, u32[]{:S(2)}, u32[]{:S(2)}) async-start(bf16[8,256,768]{2,1,0:T(8,128)(2,1)} %place_blocks.6.refs_8_), calls=%async_computation.2 | async-start | bytes 6291456 | tf_op jit(solution)/shard_map/all_to_all | solution.py:184
  119.3 3.9 %merge_rows.1.refs_7_ = bf16[4,2,256,768]{3,2,1,0:T(8,128)(2,1)} custom-call(bf16[4,2,96,768]{3,2,1,0:T(8,128)(2,1)} %bitcast.15, bf16[4,2,160,768]{3,2,1,0:T(8,128)(2,1)} %bitcast.6.refs_1_), custom_call_target="tpu_custom_call" | custom-call | tf_op jit(solution)/shard_map/merge_rows/pallas_call | solution.py:77
  123.2 11.9 %collective-permute-done.18.refs_1_ = bf16[2,256,1024]{2,1,0:T(8,128)(2,1)S(1)} collective-permute-done((bf16[2,256,1024]{2,1,0:T(8,128)(2,1)}, bf16[2,256,1024]{2,1,0:T(8,128)(2,1)S(1)}, u32[]{:S(2)}, u32[]{:S(2)}) %collective-permute-start.18) | collective-permute-done | bytes 1048608 | tf_op jit(solution)/shard_map/ppermute | solution.py:164
  145.1 11.7 %project.1 = (bf16[256,1536]{1,0:T(8,128)(2,1)}, bf16[256,1536]{1,0:T(8,128)(2,1)}, bf16[256,1536]{1,0:T(8,128)(2,1)}, bf16[256,1536]{1,0:T(8,128)(2,1)}) custom-call(bf16[2,256,1024]{2,1,0:T(8,128)(2,1)} %get-tuple-element.134.refs_0_, bf16[2,256,1024]{2,1,0:T(8,128)(2,1)} %get-tuple-element.135.refs_1_.refs_2_, ...), custom_call_target="tpu_custom_call" | custom-call | tf_op jit(solution)/shard_map/project/pallas_call | solution.py:77
  158.1 17.4 %collective-permute-done.25.refs_1_ = bf16[2,256,768]{2,1,0:T(8,128)(2,1)} collective-permute-done((bf16[2,256,768]{2,1,0:T(8,128)(2,1)}, bf16[2,256,768]{2,1,0:T(8,128)(2,1)}, u32[]{:S(2)}, u32[]{:S(2)}) %collective-permute-start.25) | collective-permute-done | bytes 786464 | tf_op jit(solution)/shard_map/ppermute | solution.py:164
  181.5 3.7 %place_blocks.7.refs_3_ = bf16[8,256,768]{2,1,0:T(8,128)(2,1)} custom-call(s32[1]{0:T(128)} %bitcast.refs_0_, bf16[2,256,768]{2,1,0:T(8,128)(2,1)} %get-tuple-element.147.refs_1_, bf16[2,256,768]{2,1,0:T(8,128)(2,1)} %collective-permute-done.31.refs_2_, bf16[2,256,768]{2,1,0:T(8,128)(2,1)} %get-tuple-element.148.refs_3_, bf16[2,256,768]{2,1,0:T(8,128)(2,1)} %copy-done.14, ...), custom_call_target="tpu_custom_call" | custom-call | tf_op jit(solution)/shard_map/place_blocks/pallas_call | solution.py:77
  185.2 4.4 %all-to-all-done.2 = bf16[8,256,768]{2,1,0:T(8,128)(2,1)} async-done(((bf16[8,256,768]{2,1,0:T(8,128)(2,1)}), bf16[8,256,768]{2,1,0:T(8,128)(2,1)}, u32[]{:S(2)}, u32[]{:S(2)}) %all-to-all-start.2) | async-done | bytes 3145760 | tf_op jit(solution)/shard_map/all_to_all | solution.py:184
  189.5 3.9 %all-to-all-start.3 = ((bf16[8,256,768]{2,1,0:T(8,128)(2,1)}), bf16[8,256,768]{2,1,0:T(8,128)(2,1)S(1)}, u32[]{:S(2)}, u32[]{:S(2)}) async-start(bf16[8,256,768]{2,1,0:T(8,128)(2,1)} %place_blocks.7.refs_3_), calls=%async_computation.3 | async-start | bytes 6291456 | tf_op jit(solution)/shard_map/all_to_all | solution.py:184
  196.8 15.7 %collective-permute-done.29.refs_1_ = bf16[256,1536]{1,0:T(8,128)(2,1)} collective-permute-done((bf16[256,1536]{1,0:T(8,128)(2,1)}, bf16[256,1536]{1,0:T(8,128)(2,1)}, u32[]{:S(2)}, u32[]{:S(2)}) %collective-permute-start.29) | collective-permute-done | bytes 786464 | tf_op jit(solution)/shard_map/ppermute | solution.py:164
  214.2 8.6 %attention.1 = (bf16[256,1536]{1,0:T(8,128)(2,1)}, bf16[256,1536]{1,0:T(8,128)(2,1)}) custom-call(s32[1]{0:T(128)S(6)} %copy.106.refs_0_, bf16[256,1536]{1,0:T(8,128)(2,1)} %get-tuple-element.143.refs_1_, bf16[256,1536]{1,0:T(8,128)(2,1)} %get-tuple-element.151.refs_2_, bf16[256,1536]{1,0:T(8,128)(2,1)} %get-tuple-element.152.refs_3_, ...), custom_call_target="tpu_custom_call" | custom-call | tf_op jit(solution)/shard_map/attention/pallas_call | solution.py:77
  225.1 17.1 %collective-permute-done.38.refs_1_.refs_2_ = bf16[256,1536]{1,0:T(8,128)(2,1)} collective-permute-done((bf16[256,1536]{1,0:T(8,128)(2,1)}, bf16[256,1536]{1,0:T(8,128)(2,1)}, u32[]{:S(2)}, u32[]{:S(2)}) %collective-permute-start.38) | collective-permute-done | bytes 786464 | tf_op jit(solution)/shard_map/ppermute | solution.py:164
  244.9 5.7 %input_terms.3 = (bf16[2,2,256,256]{3,2,1,0:T(8,128)(2,1)}, bf16[2,2,256,256]{3,2,1,0:T(8,128)(2,1)}) custom-call(s32[1]{0:T(128)} %bitcast.1.refs_0_, bf16[256,1536]{1,0:T(8,128)(2,1)} %get-tuple-element.154.refs_1_.refs_8_, bf16[4,2,256,768]{3,2,1,0:T(8,128)(2,1)} %get-tuple-element.138.refs_4_.refs_2_.refs_3_.refs_16_, bf16[4,2,256,768]{3,2,1,0:T(8,128)(2,1)} %copy-done), custom_call_target="tpu_custom_call" | custom-call | tf_op jit(solution)/shard_map/input_terms/pallas_call | solution.py:77
  250.6 7.7 %input_terms.4 = (bf16[2,4,256,256]{3,2,1,0:T(8,128)(2,1)}, bf16[2,4,256,256]{3,2,1,0:T(8,128)(2,1)}) custom-call(s32[1]{0:T(128)} %bitcast.1.refs_0_, bf16[256,1536]{1,0:T(8,128)(2,1)} %get-tuple-element.159.refs_1_.refs_10_, bf16[256,1536]{1,0:T(8,128)(2,1)} %get-tuple-element.160.refs_2_.refs_12_, ...), custom_call_target="tpu_custom_call" | custom-call | tf_op jit(solution)/shard_map/input_terms/pallas_call | solution.py:77
  264.2 5.7 %input_terms.5 = (bf16[2,2,256,256]{3,2,1,0:T(8,128)(2,1)}, bf16[2,2,256,256]{3,2,1,0:T(8,128)(2,1)}) custom-call(s32[1]{0:T(128)} %bitcast.1.refs_0_, bf16[256,1536]{1,0:T(8,128)(2,1)} %gate.19.refs_14_.refs_1_, bf16[4,2,256,768]{3,2,1,0:T(8,128)(2,1)} %get-tuple-element.138.refs_4_.refs_2_.refs_3_.refs_16_, bf16[4,2,256,768]{3,2,1,0:T(8,128)(2,1)} %copy-done), custom_call_target="tpu_custom_call" | custom-call | tf_op jit(solution)/shard_map/input_terms/pallas_call | solution.py:77
  272.0 12.1 %update.2 = (bf16[4,1,256,1536]{3,2,1,0:T(8,128)(2,1)}, f32[4,1,256,1536]{3,2,1,0:T(8,128)}, f32[4,1,256,1536]{3,2,1,0:T(8,128)}) custom-call(bf16[2,256,1024]{2,1,0:T(8,128)(2,1)} %get-tuple-element.134.refs_0_, bf16[2,256,1024]{2,1,0:T(8,128)(2,1)} %collective-permute-done.40.refs_1_, bf16[2,256,1024]{2,1,0:T(8,128)(2,1)} %get-tuple-element.135.refs_1_.refs_2_, ...), custom_call_target="tpu_custom_call" | custom-call | tf_op jit(solution)/shard_map/update/pallas_call | solution.py:378
  284.1 3.9 %collective-permute-done.39.refs_0_ = bf16[2,4,256,256]{3,2,1,0:T(8,128)(2,1)} collective-permute-done((bf16[2,4,256,256]{3,2,1,0:T(8,128)(2,1)}, bf16[2,4,256,256]{3,2,1,0:T(8,128)(2,1)}, u32[]{:S(2)}, u32[]{:S(2)}) %collective-permute-start.39) | collective-permute-done | bytes 1048608 | tf_op jit(solution)/shard_map/ppermute | solution.py:168
  295.0 12.0 %collective-permute-done.52.refs_1_ = bf16[2,2,256,256]{3,2,1,0:T(8,128)(2,1)} collective-permute-done((bf16[2,2,256,256]{3,2,1,0:T(8,128)(2,1)}, bf16[2,2,256,256]{3,2,1,0:T(8,128)(2,1)}, u32[]{:S(2)}, u32[]{:S(2)}) %collective-permute-start.52) | collective-permute-done | bytes 524320 | tf_op jit(solution)/shard_map/ppermute | solution.py:168
  309.1 6.8 %collective-permute-done.49.refs_1_ = bf16[1,4,256,256]{3,2,1,0:T(8,128)(2,1)S(1)} collective-permute-done((bf16[1,4,256,256]{3,2,1,0:T(8,128)(2,1)}, bf16[1,4,256,256]{3,2,1,0:T(8,128)(2,1)S(1)}, u32[]{:S(2)}, u32[]{:S(2)}) %collective-permute-start.49) | collective-permute-done | bytes 524320 | tf_op jit(solution)/shard_map/ppermute | solution.py:168
  321.5 3.6 %collective-permute-done.35.refs_1_ = bf16[2,2,256,256]{3,2,1,0:T(8,128)(2,1)S(1)} collective-permute-done((bf16[2,2,256,256]{3,2,1,0:T(8,128)(2,1)S(1)}, bf16[2,2,256,256]{3,2,1,0:T(8,128)(2,1)S(1)}, u32[]{:S(2)}, u32[]{:S(2)}) %collective-permute-start.35) | collective-permute-done | bytes 524320 | tf_op jit(solution)/shard_map/ppermute | solution.py:168
  328.1 12.0 %update.3 = (bf16[4,1,256,1536]{3,2,1,0:T(8,128)(2,1)}, f32[4,1,256,1536]{3,2,1,0:T(8,128)}, f32[4,1,256,1536]{3,2,1,0:T(8,128)}) custom-call(bf16[2,256,1024]{2,1,0:T(8,128)(2,1)} %get-tuple-element.134.refs_0_, bf16[2,256,1024]{2,1,0:T(8,128)(2,1)} %collective-permute-done.40.refs_1_, ...), custom_call_target="tpu_custom_call", output_to_operand_aliasing={{0}: (19, {}), {1}: (20, {}), {2}: (21, {})} | custom-call | tf_op jit(solution)/shard_map/update/pallas_call | solution.py:378
  346.9 3.4 collective-permute-done.54.refs_7_.refs_8_
  (185 shorter events, 100.8 us)
Async XLA Ops:
  23.5 22.7 %collective-permute-start.4 = (bf16[2,160,768]{2,1,0:T(8,128)(2,1)}, bf16[2,160,768]{2,1,0:T(8,128)(2,1)S(1)}, u32[]{:S(2)}, u32[]{:S(2)}) collective-permute-start(bf16[2,160,768]{2,1,0:T(8,128)(2,1)} %get-tuple-element.100), channel_id=1, source_target_pairs={{0,16},{4,20},{8,24},{12,28},{16,0},{20,4},{24,8},{28,12},{1,17},{... | collective-permute-start | bytes 1474568 | tf_op jit(solution)/shard_map/ppermute | solution.py:164
  24.4 23.3 %collective-permute-start.5 = (bf16[2,160,768]{2,1,0:T(8,128)(2,1)}, bf16[2,160,768]{2,1,0:T(8,128)(2,1)S(1)}, u32[]{:S(2)}, u32[]{:S(2)}) collective-permute-start(bf16[2,160,768]{2,1,0:T(8,128)(2,1)} %get-tuple-element.101), channel_id=1, source_target_pairs={{0,24},{4,28},{8,16},{12,20},{16,8},{20,12},{24,0},{28,4},{1,25},{... | collective-permute-start | bytes 1474568 | tf_op jit(solution)/shard_map/ppermute | solution.py:164
  27.7 24.3 %collective-permute-start.13 = (bf16[2,160,768]{2,1,0:T(8,128)(2,1)}, bf16[2,160,768]{2,1,0:T(8,128)(2,1)}, u32[]{:S(2)}, u32[]{:S(2)}) collective-permute-start(bf16[2,160,768]{2,1,0:T(8,128)(2,1)} %get-tuple-element.116.refs_1_), channel_id=1, source_target_pairs={{0,4},{4,0},{8,12},{12,8},{16,20},{20,16},{24,28},{28,24},{1,5},{5... | collective-permute-start | bytes 1474568 | tf_op jit(solution)/shard_map/ppermute | solution.py:164
  31.5 33.7 %all-to-all-start = ((bf16[8,96,768]{2,1,0:T(8,128)(2,1)}), bf16[8,96,768]{2,1,0:T(8,128)(2,1)S(1)}, u32[]{:S(2)}, u32[]{:S(2)}) async-start(bf16[8,96,768]{2,1,0:T(8,128)(2,1)} %place_blocks.4.refs_2_), calls=%async_computation | async-start | bytes 2359296 | tf_op jit(solution)/shard_map/all_to_all | solution.py:184
  48.5 21.2 %collective-permute-start.10 = (bf16[2,256,768]{2,1,0:T(8,128)(2,1)}, bf16[2,256,768]{2,1,0:T(8,128)(2,1)S(1)}, u32[]{:S(2)}, u32[]{:S(2)}) collective-permute-start(bf16[2,256,768]{2,1,0:T(8,128)(2,1)} %get-tuple-element.110), channel_id=1, source_target_pairs={{0,8},{4,12},{8,0},{12,4},{16,24},{20,28},{24,16},{28,20},{1,9},{5... | collective-permute-start | bytes 2359304 | tf_op jit(solution)/shard_map/ppermute | solution.py:164
  49.5 36.7 %collective-permute-start.11 = (bf16[2,256,768]{2,1,0:T(8,128)(2,1)}, bf16[2,256,768]{2,1,0:T(8,128)(2,1)S(1)}, u32[]{:S(2)}, u32[]{:S(2)}) collective-permute-start(bf16[2,256,768]{2,1,0:T(8,128)(2,1)} %get-tuple-element.111), channel_id=1, source_target_pairs={{0,16},{4,20},{8,24},{12,28},{16,0},{20,4},{24,8},{28,12},{1,17},{... | collective-permute-start | bytes 2359304 | tf_op jit(solution)/shard_map/ppermute | solution.py:164
  51.0 35.2 %collective-permute-start.12 = (bf16[2,256,768]{2,1,0:T(8,128)(2,1)}, bf16[2,256,768]{2,1,0:T(8,128)(2,1)S(1)}, u32[]{:S(2)}, u32[]{:S(2)}) collective-permute-start(bf16[2,256,768]{2,1,0:T(8,128)(2,1)} %get-tuple-element.112), channel_id=1, source_target_pairs={{0,24},{4,28},{8,16},{12,20},{16,8},{20,12},{24,0},{28,4},{1,25},{... | collective-permute-start | bytes 2359304 | tf_op jit(solution)/shard_map/ppermute | solution.py:164
  57.2 33.7 %collective-permute-start.20 = (bf16[2,256,768]{2,1,0:T(8,128)(2,1)}, bf16[2,256,768]{2,1,0:T(8,128)(2,1)}, u32[]{:S(2)}, u32[]{:S(2)}) collective-permute-start(bf16[2,256,768]{2,1,0:T(8,128)(2,1)} %get-tuple-element.127.refs_1_), channel_id=1, source_target_pairs={{0,4},{4,0},{8,12},{12,8},{16,20},{20,16},{24,28},{28,24},{1,5},{5... | collective-permute-start | bytes 2359304 | tf_op jit(solution)/shard_map/ppermute | solution.py:164
  65.3 49.4 %all-to-all-start.1 = ((bf16[8,160,768]{2,1,0:T(8,128)(2,1)}), bf16[8,160,768]{2,1,0:T(8,128)(2,1)}, u32[]{:S(2)}, u32[]{:S(2)}) async-start(bf16[8,160,768]{2,1,0:T(8,128)(2,1)} %place_blocks.5.refs_7_), calls=%async_computation.1 | async-start | bytes 3932160 | tf_op jit(solution)/shard_map/all_to_all | solution.py:184
  87.4 35.8 %collective-permute-start.17 = (bf16[2,256,1024]{2,1,0:T(8,128)(2,1)}, bf16[2,256,1024]{2,1,0:T(8,128)(2,1)S(1)}, u32[]{:S(2)}, u32[]{:S(2)}) collective-permute-start(bf16[2,256,1024]{2,1,0:T(8,128)(2,1)} %get-tuple-element.121), channel_id=1, source_target_pairs={{0,8},{4,12},{8,0},{12,4},{16,24},{20,28},{24,16},{28,20},{1,9},{5... | collective-permute-start | bytes 3145736 | tf_op jit(solution)/shard_map/ppermute | solution.py:164
  88.4 46.7 %collective-permute-start.18 = (bf16[2,256,1024]{2,1,0:T(8,128)(2,1)}, bf16[2,256,1024]{2,1,0:T(8,128)(2,1)S(1)}, u32[]{:S(2)}, u32[]{:S(2)}) collective-permute-start(bf16[2,256,1024]{2,1,0:T(8,128)(2,1)} %get-tuple-element.122), channel_id=1, source_target_pairs={{0,16},{4,20},{8,24},{12,28},{16,0},{20,4},{24,8},{28,12},{1,17},{... | collective-permute-start | bytes 3145736 | tf_op jit(solution)/shard_map/ppermute | solution.py:164
  89.5 47.2 %collective-permute-start.19 = (bf16[2,256,1024]{2,1,0:T(8,128)(2,1)}, bf16[2,256,1024]{2,1,0:T(8,128)(2,1)S(1)}, u32[]{:S(2)}, u32[]{:S(2)}) collective-permute-start(bf16[2,256,1024]{2,1,0:T(8,128)(2,1)} %get-tuple-element.123), channel_id=1, source_target_pairs={{0,24},{4,28},{8,16},{12,20},{16,8},{20,12},{24,0},{28,4},{1,25},{... | collective-permute-start | bytes 3145736 | tf_op jit(solution)/shard_map/ppermute | solution.py:164
  114.7 74.9 %all-to-all-start.2 = ((bf16[8,256,768]{2,1,0:T(8,128)(2,1)}), bf16[8,256,768]{2,1,0:T(8,128)(2,1)}, u32[]{:S(2)}, u32[]{:S(2)}) async-start(bf16[8,256,768]{2,1,0:T(8,128)(2,1)} %place_blocks.6.refs_8_), calls=%async_computation.2 | async-start | bytes 6291456 | tf_op jit(solution)/shard_map/all_to_all | solution.py:184
  137.6 20.5 %collective-permute-start.24 = (bf16[2,256,768]{2,1,0:T(8,128)(2,1)}, bf16[2,256,768]{2,1,0:T(8,128)(2,1)S(1)}, u32[]{:S(2)}, u32[]{:S(2)}) collective-permute-start(bf16[2,256,768]{2,1,0:T(8,128)(2,1)} %get-tuple-element.131), channel_id=1, source_target_pairs={{0,8},{4,12},{8,0},{12,4},{16,24},{20,28},{24,16},{28,20},{1,9},{5... | collective-permute-start | bytes 2359304 | tf_op jit(solution)/shard_map/ppermute | solution.py:164
  138.7 36.8 %collective-permute-start.25 = (bf16[2,256,768]{2,1,0:T(8,128)(2,1)}, bf16[2,256,768]{2,1,0:T(8,128)(2,1)}, u32[]{:S(2)}, u32[]{:S(2)}) collective-permute-start(bf16[2,256,768]{2,1,0:T(8,128)(2,1)} %get-tuple-element.132), channel_id=1, source_target_pairs={{0,16},{4,20},{8,24},{12,28},{16,0},{20,4},{24,8},{28,12},{1,17},{... | collective-permute-start | bytes 2359304 | tf_op jit(solution)/shard_map/ppermute | solution.py:164
  140.3 35.3 %collective-permute-start.26 = (bf16[2,256,768]{2,1,0:T(8,128)(2,1)}, bf16[2,256,768]{2,1,0:T(8,128)(2,1)}, u32[]{:S(2)}, u32[]{:S(2)}) collective-permute-start(bf16[2,256,768]{2,1,0:T(8,128)(2,1)} %get-tuple-element.133), channel_id=1, source_target_pairs={{0,24},{4,28},{8,16},{12,20},{16,8},{20,12},{24,0},{28,4},{1,25},{... | collective-permute-start | bytes 2359304 | tf_op jit(solution)/shard_map/ppermute | solution.py:164
  141.1 36.3 %collective-permute-start.31 = (bf16[2,256,768]{2,1,0:T(8,128)(2,1)}, bf16[2,256,768]{2,1,0:T(8,128)(2,1)}, u32[]{:S(2)}, u32[]{:S(2)}) collective-permute-start(bf16[2,256,768]{2,1,0:T(8,128)(2,1)} %get-tuple-element.147.refs_1_), channel_id=1, source_target_pairs={{0,4},{4,0},{8,12},{12,8},{16,20},{20,16},{24,28},{28,24},{1,5},{5... | collective-permute-start | bytes 2359304 | tf_op jit(solution)/shard_map/ppermute | solution.py:164
  176.2 20.7 %collective-permute-start.28 = (bf16[256,1536]{1,0:T(8,128)(2,1)}, bf16[256,1536]{1,0:T(8,128)(2,1)}, u32[]{:S(2)}, u32[]{:S(2)}) collective-permute-start(bf16[256,1536]{1,0:T(8,128)(2,1)} %get-tuple-element.144), channel_id=1, source_target_pairs={{0,8},{4,12},{8,0},{12,4},{16,24},{20,28},{24,16},{28,20},{1,9},{5... | collective-permute-start | bytes 2359304 | tf_op jit(solution)/shard_map/ppermute | solution.py:164
  177.3 35.2 %collective-permute-start.29 = (bf16[256,1536]{1,0:T(8,128)(2,1)}, bf16[256,1536]{1,0:T(8,128)(2,1)}, u32[]{:S(2)}, u32[]{:S(2)}) collective-permute-start(bf16[256,1536]{1,0:T(8,128)(2,1)} %get-tuple-element.145), channel_id=1, source_target_pairs={{0,16},{4,20},{8,24},{12,28},{16,0},{20,4},{24,8},{28,12},{1,17},{... | collective-permute-start | bytes 2359304 | tf_op jit(solution)/shard_map/ppermute | solution.py:164
  178.2 35.9 %collective-permute-start.30 = (bf16[256,1536]{1,0:T(8,128)(2,1)}, bf16[256,1536]{1,0:T(8,128)(2,1)}, u32[]{:S(2)}, u32[]{:S(2)}) collective-permute-start(bf16[256,1536]{1,0:T(8,128)(2,1)} %get-tuple-element.146), channel_id=1, source_target_pairs={{0,24},{4,28},{8,16},{12,20},{16,8},{20,12},{24,0},{28,4},{1,25},{... | collective-permute-start | bytes 2359304 | tf_op jit(solution)/shard_map/ppermute | solution.py:164
  189.5 80.8 %all-to-all-start.3 = ((bf16[8,256,768]{2,1,0:T(8,128)(2,1)}), bf16[8,256,768]{2,1,0:T(8,128)(2,1)S(1)}, u32[]{:S(2)}, u32[]{:S(2)}) async-start(bf16[8,256,768]{2,1,0:T(8,128)(2,1)} %place_blocks.7.refs_3_), calls=%async_computation.3 | async-start | bytes 6291456 | tf_op jit(solution)/shard_map/all_to_all | solution.py:184
  222.7 19.4 %collective-permute-start.38 = (bf16[256,1536]{1,0:T(8,128)(2,1)}, bf16[256,1536]{1,0:T(8,128)(2,1)}, u32[]{:S(2)}, u32[]{:S(2)}) collective-permute-start(bf16[256,1536]{1,0:T(8,128)(2,1)} %get-tuple-element.154.refs_1_.refs_8_), channel_id=1, source_target_pairs={{0,16},{4,20},{8,24},{12,28},{16,0},{20,4},{24,8},{28,12},{1,17},{... | collective-permute-start | bytes 2359304 | tf_op jit(solution)/shard_map/ppermute | solution.py:164
  243.9 19.2 %collective-permute-start.41 = (bf16[2,256,1024]{2,1,0:T(8,128)(2,1)}, bf16[2,256,1024]{2,1,0:T(8,128)(2,1)}, u32[]{:S(2)}, u32[]{:S(2)}) collective-permute-start(bf16[2,256,1024]{2,1,0:T(8,128)(2,1)} %get-tuple-element.135.refs_1_.refs_2_), channel_id=1, source_target_pairs={{0,4},{4,0},{8,12},{12,8},{16,20},{20,16},{24,28},{28,24},{1,5},{5... | collective-permute-start | bytes 3145736 | tf_op jit(solution)/shard_map/ppermute | solution.py:164
  244.4 19.2 %collective-permute-start.42 = (bf16[2,256,1024]{2,1,0:T(8,128)(2,1)}, bf16[2,256,1024]{2,1,0:T(8,128)(2,1)}, u32[]{:S(2)}, u32[]{:S(2)}) collective-permute-start(bf16[2,256,1024]{2,1,0:T(8,128)(2,1)} %get-tuple-element.136.refs_2_.refs_4_), channel_id=1, source_target_pairs={{0,4},{4,0},{8,12},{12,8},{16,20},{20,16},{24,28},{28,24},{1,5},{5... | collective-permute-start | bytes 3145736 | tf_op jit(solution)/shard_map/ppermute | solution.py:164
  244.4 19.3 %collective-permute-start.43 = (bf16[2,256,1024]{2,1,0:T(8,128)(2,1)}, bf16[2,256,1024]{2,1,0:T(8,128)(2,1)}, u32[]{:S(2)}, u32[]{:S(2)}) collective-permute-start(bf16[2,256,1024]{2,1,0:T(8,128)(2,1)} %get-tuple-element.137.refs_3_.refs_6_), channel_id=1, source_target_pairs={{0,4},{4,0},{8,12},{12,8},{16,20},{20,16},{24,28},{28,24},{1,5},{5... | collective-permute-start | bytes 3145736 | tf_op jit(solution)/shard_map/ppermute | solution.py:164
  261.6 26.4 %collective-permute-start.39 = (bf16[2,4,256,256]{3,2,1,0:T(8,128)(2,1)}, bf16[2,4,256,256]{3,2,1,0:T(8,128)(2,1)}, u32[]{:S(2)}, u32[]{:S(2)}) collective-permute-start(bf16[2,4,256,256]{3,2,1,0:T(8,128)(2,1)} %get-tuple-element.162), channel_id=1, source_target_pairs={{0,1},{1,0},{2,3},{3,2},{4,5},{5,4},{6,7},{7,6},{8,9},{9,8},{10,11... | collective-permute-start | bytes 3145736 | tf_op jit(solution)/shard_map/ppermute | solution.py:168
  269.9 37.1 %collective-permute-start.52 = (bf16[2,2,256,256]{3,2,1,0:T(8,128)(2,1)}, bf16[2,2,256,256]{3,2,1,0:T(8,128)(2,1)}, u32[]{:S(2)}, u32[]{:S(2)}) collective-permute-start(bf16[2,2,256,256]{3,2,1,0:T(8,128)(2,1)} %get-tuple-element.170), channel_id=1, source_target_pairs={{0,1},{1,0},{2,3},{3,2},{4,5},{5,4},{6,7},{7,6},{8,9},{9,8},{10,11... | collective-permute-start | bytes 1572872 | tf_op jit(solution)/shard_map/ppermute | solution.py:168
  290.8 25.1 %collective-permute-start.49 = (bf16[1,4,256,256]{3,2,1,0:T(8,128)(2,1)}, bf16[1,4,256,256]{3,2,1,0:T(8,128)(2,1)S(1)}, u32[]{:S(2)}, u32[]{:S(2)}) collective-permute-start(bf16[1,4,256,256]{3,2,1,0:T(8,128)(2,1)} %get-tuple-element.166), channel_id=1, source_target_pairs={{0,2},{1,3},{2,0},{3,1},{4,6},{5,7},{6,4},{7,5},{8,10},{9,11},{10,... | collective-permute-start | bytes 1572872 | tf_op jit(solution)/shard_map/ppermute | solution.py:168
  293.4 31.8 %collective-permute-start.35 = (bf16[2,2,256,256]{3,2,1,0:T(8,128)(2,1)S(1)}, bf16[2,2,256,256]{3,2,1,0:T(8,128)(2,1)S(1)}, u32[]{:S(2)}, u32[]{:S(2)}) collective-permute-start(bf16[2,2,256,256]{3,2,1,0:T(8,128)(2,1)S(1)} %copy-done.31), channel_id=1, source_target_pairs={{0,1},{1,0},{2,3},{3,2},{4,5},{5,4},{6,7},{7,6},{8,9},{9,8},{10,11... | collective-permute-start | bytes 1572872 | tf_op jit(solution)/shard_map/ppermute | solution.py:168
  309.1 30.9 %collective-permute-start.53 = (bf16[1,2,256,256]{3,2,1,0:T(8,128)(2,1)}, bf16[1,2,256,256]{3,2,1,0:T(8,128)(2,1)S(1)}, u32[]{:S(2)}, u32[]{:S(2)}) collective-permute-start(bf16[1,2,256,256]{3,2,1,0:T(8,128)(2,1)} %get-tuple-element.172), channel_id=1, source_target_pairs={{0,2},{1,3},{2,0},{3,1},{4,6},{5,7},{6,4},{7,5},{8,10},{9,11},{10,... | collective-permute-start | bytes 786440 | tf_op jit(solution)/shard_map/ppermute | solution.py:168
  318.9 21.2 %collective-permute-start.51 = (bf16[2,256,256]{2,1,0:T(8,128)(2,1)}, bf16[2,256,256]{2,1,0:T(8,128)(2,1)S(1)}, u32[]{:S(2)}, u32[]{:S(2)}) collective-permute-start(bf16[2,256,256]{2,1,0:T(8,128)(2,1)} %get-tuple-element.168), channel_id=1, source_target_pairs={{0,16},{4,20},{8,24},{12,28},{16,0},{20,4},{24,8},{28,12},{1,17},{... | collective-permute-start | bytes 786440 | tf_op jit(solution)/shard_map/ppermute | solution.py:164
  320.6 19.5 %collective-permute-start.50 = (bf16[2,256,256]{2,1,0:T(8,128)(2,1)}, bf16[2,256,256]{2,1,0:T(8,128)(2,1)S(1)}, u32[]{:S(2)}, u32[]{:S(2)}) collective-permute-start(bf16[2,256,256]{2,1,0:T(8,128)(2,1)} %get-tuple-element.167.refs_22_), channel_id=1, source_target_pairs={{0,8},{4,12},{8,0},{12,4},{16,24},{20,28},{24,16},{28,20},{1,9},{5... | collective-permute-start | bytes 786440 | tf_op jit(solution)/shard_map/ppermute | solution.py:164
  (59 other events, 353.1 us)

commit v3 on v2

--- a/solution.py
+++ b/solution.py
@@ -174,10 +174,6 @@
 
 def to_cores(pairs):
     return [view for x in pairs for view in ((x, 0), (swap(x, 1), 1))]
-
-
-def exchange(pieces):
-    return [swap(piece, k) for k, piece in enumerate(pieces)]
 
 
 def over_tensor(x):
@@ -436,12 +432,10 @@
         return kept, received
 
     near = [swap(columns, 2 * m) for m in range(1, chips - 1)]
-    far = swap(gate([columns_again], near)[0] if 1 else columns, 2 * (chips - 1))
     own_state = begin([columns])
-    near = gate(near, own_state[:1], 8)
+    far = swap(gate([columns_again], [*near, own_state[0]])[0], 2 * (chips - 1))
+    near = gate(near, (), 8)
     near_state = begin(near)
-    if 0:
-        own_state = proceed(*own_state)
     (far,) = gate([far], [own_state[0], near_state[0]], 8)
     far_state = begin([far])
     same_core = [columns, *near, far]
@@ -450,11 +444,10 @@
     some = update(*operands, 0, tensor_count // 2)
     own_state = proceed(*own_state)
     near_state = proceed(near_state[0], gate(near_state[1:], some[:1])[0])
-    far_state = proceed(*far_state)
-    near_sums = sum_terms(*near_state)
-    new_weights, new_first, new_second = update(*operands, tensor_count // 2, tensor_count, some, near_sums[:1])
-    near_sums = [swap(x, 2 * m + 2) for m, x in enumerate(near_sums)]
-    (far_sum,) = sum_terms(far_state[0], gate(far_state[1:], [new_weights, *near_sums])[0])
+    new_weights, new_first, new_second = update(*operands, tensor_count // 2, tensor_count, some, near_state[:1])
+    far_state = proceed(far_state[0], gate(far_state[1:], [new_weights])[0])
+    near_sums = [swap(x, 2 * m + 2) for m, x in enumerate(sum_terms(*near_state))]
+    (far_sum,) = sum_terms(far_state[0], gate(far_state[1:], near_sums)[0])
     pairs = [*sum_terms(*own_state), *near_sums, swap(far_sum, 2 * (chips - 1))]
     input_grad = place_columns(me, [(x, at) for x in pairs for at in range(2)], (new_weights,))
     return (input_grad, new_weights, new_first, new_second)

time: 354 us -> 347 us (0.980)
  waiting for transfers between devices: 164 us -> 155 us
    ppermute x6, waiting for transfers between devices: 26.3 us -> 20.8 us  [swap_tensor(): lax.ppermute(x, 'tensor', [(i, i ^ j) for i in range(lax.axis_size('tenso...]
  transfers between devices with their start and end apart: 59 -> 59, of which waited for: 28 -> 27; matrix products, arithmetic and copies ran while one was open for 0% -> 0% of each run, Pallas kernels for 31% -> 32%
where the time goes in v3:
time: 347 us; the launch traced here: 346 us
  waiting for transfers between devices  155 us (45%)
  Pallas kernels  117 us (34%)
  starting transfers between devices  58.8 us (17%)
  local copies, waits for them, and re-layouts  13.6 us (4%)
    ppermute x49, waiting for transfers between devices, swap(): lax.ppermute(x, 'dp', [(i, i ^ k) for i in range(lax.axis_size('dp'))])  109 us
    pallas_call x22, Pallas kernels, whole_call(): return list(call(*arrays, *waits))  92.2 us
    ppermute x49, starting transfers between devices, swap(): lax.ppermute(x, 'dp', [(i, i ^ k) for i in range(lax.axis_size('dp'))])  34.4 us
    all_to_all x4, waiting for transfers between devices, over_tensor(): return lax.all_to_all(x, 'tensor', split_axis=0, concat_axis=0, tiled=True)  25.6 us
    pallas_call x2, Pallas kernels, update(): return list(call(*ins))  24.3 us
    ppermute x6, waiting for transfers between devices, swap_tensor(): lax.ppermute(x, 'tensor', [(i, i ^ j) for i in range(lax.axis_size('tenso...  20.8 us
    all_to_all x4, starting transfers between devices, over_tensor(): return lax.all_to_all(x, 'tensor', split_axis=0, concat_axis=0, tiled=True)  17.8 us
    unnamed x64, local copies, waits for them, and re-layouts  13.6 us
  transfers between devices with their start and end apart: 59, of which 27 were waited for; matrix products, arithmetic and copies ran while one was open for 0% of the time, Pallas kernels for 32%

profile of v3, /device:TPU:0, one launch (start us, length us, event | category | flops | bytes accessed | tf_op | source)
XLA Modules:
  0.0 345.8 jit_solution(7371485074805833755)
XLA Ops:
  11.4 4.7 %pack_blocks.6 = (bf16[2,256,768]{2,1,0:T(8,128)(2,1)}, bf16[2,256,768]{2,1,0:T(8,128)(2,1)}, bf16[2,256,768]{2,1,0:T(8,128)(2,1)}, bf16[2,256,768]{2,1,0:T(8,128)(2,1)}) custom-call(s32[1]{0:T(128)} %bitcast.refs_0_, f32[8,256,768]{2,1,0:T(8,128)} %bitcast.13), custom_call_target="tpu_custom_call" | custom-call | tf_op jit(solution)/shard_map/pack_blocks/pallas_call | solution.py:77
  16.1 5.4 %collective-permute-done.1.refs_1_ = bf16[2,96,768]{2,1,0:T(8,128)(2,1)S(1)} collective-permute-done((bf16[2,96,768]{2,1,0:T(8,128)(2,1)}, bf16[2,96,768]{2,1,0:T(8,128)(2,1)S(1)}, u32[]{:S(2)}, u32[]{:S(2)}) %collective-permute-start.1) | collective-permute-done | bytes 294944 | tf_op jit(solution)/shard_map/ppermute | solution.py:164
  31.5 4.9 %all-to-all-start = ((bf16[8,96,768]{2,1,0:T(8,128)(2,1)}), bf16[8,96,768]{2,1,0:T(8,128)(2,1)S(1)}, u32[]{:S(2)}, u32[]{:S(2)}) async-start(bf16[8,96,768]{2,1,0:T(8,128)(2,1)} %place_blocks.4.refs_2_), calls=%async_computation | async-start | bytes 2359296 | tf_op jit(solution)/shard_map/all_to_all | solution.py:180
  36.4 4.9 %pack_columns.1 = (bf16[2,256,1024]{2,1,0:T(8,128)(2,1)}, bf16[2,256,1024]{2,1,0:T(8,128)(2,1)}, bf16[2,256,1024]{2,1,0:T(8,128)(2,1)}, bf16[2,256,1024]{2,1,0:T(8,128)(2,1)}) custom-call(s32[1]{0:T(128)} %bitcast.refs_0_, bf16[256,8192]{1,0:T(8,128)(2,1)} %refs_1_.1, bf16[8,96,768]{2,1,0:T(8,128)(2,1)} %place_blocks.4.refs_2_), custom_call_target="tpu_custom_call" | custom-call | tf_op jit(solution)/shard_map/pack_columns/pallas_call | solution.py:77
  41.3 4.9 %collective-permute-done.4.refs_1_ = bf16[2,160,768]{2,1,0:T(8,128)(2,1)S(1)} collective-permute-done((bf16[2,160,768]{2,1,0:T(8,128)(2,1)}, bf16[2,160,768]{2,1,0:T(8,128)(2,1)S(1)}, u32[]{:S(2)}, u32[]{:S(2)}) %collective-permute-start.4) | collective-permute-done | bytes 491552 | tf_op jit(solution)/shard_map/ppermute | solution.py:164
  52.5 4.7 %pack_blocks.7 = (bf16[2,256,768]{2,1,0:T(8,128)(2,1)}, bf16[2,256,768]{2,1,0:T(8,128)(2,1)}, bf16[2,256,768]{2,1,0:T(8,128)(2,1)}, bf16[2,256,768]{2,1,0:T(8,128)(2,1)}) custom-call(s32[1]{0:T(128)} %bitcast.refs_0_, f32[8,256,768]{2,1,0:T(8,128)} %bitcast.14), custom_call_target="tpu_custom_call" | custom-call | tf_op jit(solution)/shard_map/pack_blocks/pallas_call | solution.py:77
  60.5 4.7 %all-to-all-done = bf16[8,96,768]{2,1,0:T(8,128)(2,1)S(1)} async-done(((bf16[8,96,768]{2,1,0:T(8,128)(2,1)}), bf16[8,96,768]{2,1,0:T(8,128)(2,1)S(1)}, u32[]{:S(2)}, u32[]{:S(2)}) %all-to-all-start) | async-done | bytes 1179680 | tf_op jit(solution)/shard_map/all_to_all | solution.py:180
  65.2 4.4 %all-to-all-start.1 = ((bf16[8,160,768]{2,1,0:T(8,128)(2,1)}), bf16[8,160,768]{2,1,0:T(8,128)(2,1)}, u32[]{:S(2)}, u32[]{:S(2)}) async-start(bf16[8,160,768]{2,1,0:T(8,128)(2,1)} %place_blocks.5.refs_7_), calls=%async_computation.1 | async-start | bytes 3932160 | tf_op jit(solution)/shard_map/all_to_all | solution.py:180
  69.7 16.5 %collective-permute-done.11.refs_1_ = bf16[2,256,768]{2,1,0:T(8,128)(2,1)S(1)} collective-permute-done((bf16[2,256,768]{2,1,0:T(8,128)(2,1)}, bf16[2,256,768]{2,1,0:T(8,128)(2,1)S(1)}, u32[]{:S(2)}, u32[]{:S(2)}) %collective-permute-start.11) | collective-permute-done | bytes 786464 | tf_op jit(solution)/shard_map/ppermute | solution.py:164
  94.6 3.7 %place_blocks.6.refs_8_ = bf16[8,256,768]{2,1,0:T(8,128)(2,1)} custom-call(s32[1]{0:T(128)} %bitcast.refs_0_, bf16[2,256,768]{2,1,0:T(8,128)(2,1)} %get-tuple-element.127.refs_1_, bf16[2,256,768]{2,1,0:T(8,128)(2,1)} %collective-permute-done.20.refs_2_, bf16[2,256,768]{2,1,0:T(8,128)(2,1)} %get-tuple-element.128.refs_3_, ...), custom_call_target="tpu_custom_call" | custom-call | tf_op jit(solution)/shard_map/place_blocks/pallas_call | solution.py:77
  98.3 16.4 %all-to-all-done.1 = bf16[8,160,768]{2,1,0:T(8,128)(2,1)} async-done(((bf16[8,160,768]{2,1,0:T(8,128)(2,1)}), bf16[8,160,768]{2,1,0:T(8,128)(2,1)}, u32[]{:S(2)}, u32[]{:S(2)}) %all-to-all-start.1) | async-done | bytes 1966112 | tf_op jit(solution)/shard_map/all_to_all | solution.py:180
  114.7 4.6 %all-to-all-start.2 = ((bf16[8,256,768]{2,1,0:T(8,128)(2,1)}), bf16[8,256,768]{2,1,0:T(8,128)(2,1)}, u32[]{:S(2)}, u32[]{:S(2)}) async-start(bf16[8,256,768]{2,1,0:T(8,128)(2,1)} %place_blocks.6.refs_8_), calls=%async_computation.2 | async-start | bytes 6291456 | tf_op jit(solution)/shard_map/all_to_all | solution.py:180
  119.3 3.9 %merge_rows.1.refs_7_ = bf16[4,2,256,768]{3,2,1,0:T(8,128)(2,1)} custom-call(bf16[4,2,96,768]{3,2,1,0:T(8,128)(2,1)} %bitcast.15, bf16[4,2,160,768]{3,2,1,0:T(8,128)(2,1)} %bitcast.6.refs_1_), custom_call_target="tpu_custom_call" | custom-call | tf_op jit(solution)/shard_map/merge_rows/pallas_call | solution.py:77
  123.2 11.8 %collective-permute-done.18.refs_1_ = bf16[2,256,1024]{2,1,0:T(8,128)(2,1)S(1)} collective-permute-done((bf16[2,256,1024]{2,1,0:T(8,128)(2,1)}, bf16[2,256,1024]{2,1,0:T(8,128)(2,1)S(1)}, u32[]{:S(2)}, u32[]{:S(2)}) %collective-permute-start.18) | collective-permute-done | bytes 1048608 | tf_op jit(solution)/shard_map/ppermute | solution.py:164
  145.1 11.6 %project.1 = (bf16[256,1536]{1,0:T(8,128)(2,1)}, bf16[256,1536]{1,0:T(8,128)(2,1)}, bf16[256,1536]{1,0:T(8,128)(2,1)}, bf16[256,1536]{1,0:T(8,128)(2,1)}) custom-call(bf16[2,256,1024]{2,1,0:T(8,128)(2,1)} %get-tuple-element.134.refs_0_, bf16[2,256,1024]{2,1,0:T(8,128)(2,1)} %get-tuple-element.135.refs_1_.refs_2_, ...), custom_call_target="tpu_custom_call" | custom-call | tf_op jit(solution)/shard_map/project/pallas_call | solution.py:77
  158.1 17.4 %collective-permute-done.25.refs_1_ = bf16[2,256,768]{2,1,0:T(8,128)(2,1)} collective-permute-done((bf16[2,256,768]{2,1,0:T(8,128)(2,1)}, bf16[2,256,768]{2,1,0:T(8,128)(2,1)}, u32[]{:S(2)}, u32[]{:S(2)}) %collective-permute-start.25) | collective-permute-done | bytes 786464 | tf_op jit(solution)/shard_map/ppermute | solution.py:164
  181.4 3.7 %place_blocks.7.refs_3_ = bf16[8,256,768]{2,1,0:T(8,128)(2,1)} custom-call(s32[1]{0:T(128)} %bitcast.refs_0_, bf16[2,256,768]{2,1,0:T(8,128)(2,1)} %get-tuple-element.147.refs_1_, bf16[2,256,768]{2,1,0:T(8,128)(2,1)} %collective-permute-done.31.refs_2_, bf16[2,256,768]{2,1,0:T(8,128)(2,1)} %get-tuple-element.148.refs_3_, bf16[2,256,768]{2,1,0:T(8,128)(2,1)} %copy-done.14, ...), custom_call_target="tpu_custom_call" | custom-call | tf_op jit(solution)/shard_map/place_blocks/pallas_call | solution.py:77
  185.1 4.5 %all-to-all-done.2 = bf16[8,256,768]{2,1,0:T(8,128)(2,1)} async-done(((bf16[8,256,768]{2,1,0:T(8,128)(2,1)}), bf16[8,256,768]{2,1,0:T(8,128)(2,1)}, u32[]{:S(2)}, u32[]{:S(2)}) %all-to-all-start.2) | async-done | bytes 3145760 | tf_op jit(solution)/shard_map/all_to_all | solution.py:180
  189.5 3.9 %all-to-all-start.3 = ((bf16[8,256,768]{2,1,0:T(8,128)(2,1)}), bf16[8,256,768]{2,1,0:T(8,128)(2,1)S(1)}, u32[]{:S(2)}, u32[]{:S(2)}) async-start(bf16[8,256,768]{2,1,0:T(8,128)(2,1)} %place_blocks.7.refs_3_), calls=%async_computation.3 | async-start | bytes 6291456 | tf_op jit(solution)/shard_map/all_to_all | solution.py:180
  196.7 15.7 %collective-permute-done.29.refs_1_ = bf16[256,1536]{1,0:T(8,128)(2,1)} collective-permute-done((bf16[256,1536]{1,0:T(8,128)(2,1)}, bf16[256,1536]{1,0:T(8,128)(2,1)}, u32[]{:S(2)}, u32[]{:S(2)}) %collective-permute-start.29) | collective-permute-done | bytes 786464 | tf_op jit(solution)/shard_map/ppermute | solution.py:164
  214.1 8.6 %attention.1 = (bf16[256,1536]{1,0:T(8,128)(2,1)}, bf16[256,1536]{1,0:T(8,128)(2,1)}) custom-call(s32[1]{0:T(128)S(6)} %copy.108.refs_0_, bf16[256,1536]{1,0:T(8,128)(2,1)} %get-tuple-element.143.refs_1_, bf16[256,1536]{1,0:T(8,128)(2,1)} %get-tuple-element.151.refs_2_, bf16[256,1536]{1,0:T(8,128)(2,1)} %get-tuple-element.152.refs_3_, ...), custom_call_target="tpu_custom_call" | custom-call | tf_op jit(solution)/shard_map/attention/pallas_call | solution.py:77
  225.0 5.7 %input_terms.3 = (bf16[2,2,256,256]{3,2,1,0:T(8,128)(2,1)}, bf16[2,2,256,256]{3,2,1,0:T(8,128)(2,1)}) custom-call(s32[1]{0:T(128)} %bitcast.1.refs_0_, bf16[256,1536]{1,0:T(8,128)(2,1)} %get-tuple-element.154.refs_1_.refs_8_, bf16[4,2,256,768]{3,2,1,0:T(8,128)(2,1)} %get-tuple-element.138.refs_4_.refs_2_.refs_3_.refs_16_, bf16[4,2,256,768]{3,2,1,0:T(8,128)(2,1)} %copy-done), custom_call_target="tpu_custom_call" | custom-call | tf_op jit(solution)/shard_map/input_terms/pallas_call | solution.py:77
  230.7 11.4 %collective-permute-done.38.refs_1_.refs_2_ = bf16[256,1536]{1,0:T(8,128)(2,1)} collective-permute-done((bf16[256,1536]{1,0:T(8,128)(2,1)}, bf16[256,1536]{1,0:T(8,128)(2,1)}, u32[]{:S(2)}, u32[]{:S(2)}) %collective-permute-start.38) | collective-permute-done | bytes 786464 | tf_op jit(solution)/shard_map/ppermute | solution.py:164
  244.8 7.8 %input_terms.4 = (bf16[2,4,256,256]{3,2,1,0:T(8,128)(2,1)}, bf16[2,4,256,256]{3,2,1,0:T(8,128)(2,1)}) custom-call(s32[1]{0:T(128)} %bitcast.1.refs_0_, bf16[256,1536]{1,0:T(8,128)(2,1)} %get-tuple-element.159.refs_1_.refs_10_, bf16[256,1536]{1,0:T(8,128)(2,1)} %get-tuple-element.160.refs_2_.refs_12_, ...), custom_call_target="tpu_custom_call" | custom-call | tf_op jit(solution)/shard_map/input_terms/pallas_call | solution.py:77
  252.6 8.9 %collective-permute-done.47.refs_0_ = bf16[256,1536]{1,0:T(8,128)(2,1)} collective-permute-done((bf16[256,1536]{1,0:T(8,128)(2,1)}, bf16[256,1536]{1,0:T(8,128)(2,1)}, u32[]{:S(2)}, u32[]{:S(2)}) %collective-permute-start.47) | collective-permute-done | bytes 786464 | tf_op jit(solution)/shard_map/ppermute | solution.py:164
  264.1 5.8 %input_terms.5 = (bf16[2,2,256,256]{3,2,1,0:T(8,128)(2,1)}, bf16[2,2,256,256]{3,2,1,0:T(8,128)(2,1)}) custom-call(s32[1]{0:T(128)} %bitcast.1.refs_0_, bf16[256,1536]{1,0:T(8,128)(2,1)} %gate.20.refs_14_.refs_1_, bf16[4,2,256,768]{3,2,1,0:T(8,128)(2,1)} %get-tuple-element.138.refs_4_.refs_2_.refs_3_.refs_16_, bf16[4,2,256,768]{3,2,1,0:T(8,128)(2,1)} %copy-done), custom_call_target="tpu_custom_call" | custom-call | tf_op jit(solution)/shard_map/input_terms/pallas_call | solution.py:77
  271.9 12.1 %update.2 = (bf16[4,1,256,1536]{3,2,1,0:T(8,128)(2,1)}, f32[4,1,256,1536]{3,2,1,0:T(8,128)}, f32[4,1,256,1536]{3,2,1,0:T(8,128)}) custom-call(bf16[2,256,1024]{2,1,0:T(8,128)(2,1)} %get-tuple-element.134.refs_0_, bf16[2,256,1024]{2,1,0:T(8,128)(2,1)} %collective-permute-done.40.refs_1_, bf16[2,256,1024]{2,1,0:T(8,128)(2,1)} %get-tuple-element.135.refs_1_.refs_2_, ...), custom_call_target="tpu_custom_call" | custom-call | tf_op jit(solution)/shard_map/update/pallas_call | solution.py:374
  284.0 3.8 %collective-permute-done.39.refs_0_ = bf16[2,4,256,256]{3,2,1,0:T(8,128)(2,1)} collective-permute-done((bf16[2,4,256,256]{3,2,1,0:T(8,128)(2,1)}, bf16[2,4,256,256]{3,2,1,0:T(8,128)(2,1)}, u32[]{:S(2)}, u32[]{:S(2)}) %collective-permute-start.39) | collective-permute-done | bytes 1048608 | tf_op jit(solution)/shard_map/ppermute | solution.py:168
  294.9 12.2 %update.3 = (bf16[4,1,256,1536]{3,2,1,0:T(8,128)(2,1)}, f32[4,1,256,1536]{3,2,1,0:T(8,128)}, f32[4,1,256,1536]{3,2,1,0:T(8,128)}) custom-call(bf16[2,256,1024]{2,1,0:T(8,128)(2,1)} %get-tuple-element.134.refs_0_, bf16[2,256,1024]{2,1,0:T(8,128)(2,1)} %collective-permute-done.40.refs_1_, ...), custom_call_target="tpu_custom_call", output_to_operand_aliasing={{0}: (19, {}), {1}: (20, {}), {2}: (21, {})} | custom-call | tf_op jit(solution)/shard_map/update/pallas_call | solution.py:374
  309.6 6.3 %collective-permute-done.49.refs_1_ = bf16[1,4,256,256]{3,2,1,0:T(8,128)(2,1)S(1)} collective-permute-done((bf16[1,4,256,256]{3,2,1,0:T(8,128)(2,1)}, bf16[1,4,256,256]{3,2,1,0:T(8,128)(2,1)S(1)}, u32[]{:S(2)}, u32[]{:S(2)}) %collective-permute-start.49) | collective-permute-done | bytes 524320 | tf_op jit(solution)/shard_map/ppermute | solution.py:168
  321.8 3.4 collective-permute-done.35.refs_1_
  332.9 7.2 %collective-permute-done.36.refs_1_ = bf16[1,2,256,256]{3,2,1,0:T(8,128)(2,1)S(1)} collective-permute-done((bf16[1,2,256,256]{3,2,1,0:T(8,128)(2,1)}, bf16[1,2,256,256]{3,2,1,0:T(8,128)(2,1)S(1)}, u32[]{:S(2)}, u32[]{:S(2)}) %collective-permute-start.36) | collective-permute-done | bytes 262176 | tf_op jit(solution)/shard_map/ppermute | solution.py:168
  (186 shorter events, 98.7 us)
Async XLA Ops:
  22.4 18.9 %collective-permute-start.3 = (bf16[2,160,768]{2,1,0:T(8,128)(2,1)}, bf16[2,160,768]{2,1,0:T(8,128)(2,1)S(1)}, u32[]{:S(2)}, u32[]{:S(2)}) collective-permute-start(bf16[2,160,768]{2,1,0:T(8,128)(2,1)} %get-tuple-element.99), channel_id=1, source_target_pairs={{0,8},{4,12},{8,0},{12,4},{16,24},{20,28},{24,16},{28,20},{1,9},{5... | collective-permute-start | bytes 1474568 | tf_op jit(solution)/shard_map/ppermute | solution.py:164
  23.5 22.7 %collective-permute-start.4 = (bf16[2,160,768]{2,1,0:T(8,128)(2,1)}, bf16[2,160,768]{2,1,0:T(8,128)(2,1)S(1)}, u32[]{:S(2)}, u32[]{:S(2)}) collective-permute-start(bf16[2,160,768]{2,1,0:T(8,128)(2,1)} %get-tuple-element.100), channel_id=1, source_target_pairs={{0,16},{4,20},{8,24},{12,28},{16,0},{20,4},{24,8},{28,12},{1,17},{... | collective-permute-start | bytes 1474568 | tf_op jit(solution)/shard_map/ppermute | solution.py:164
  24.4 23.3 %collective-permute-start.5 = (bf16[2,160,768]{2,1,0:T(8,128)(2,1)}, bf16[2,160,768]{2,1,0:T(8,128)(2,1)S(1)}, u32[]{:S(2)}, u32[]{:S(2)}) collective-permute-start(bf16[2,160,768]{2,1,0:T(8,128)(2,1)} %get-tuple-element.101), channel_id=1, source_target_pairs={{0,24},{4,28},{8,16},{12,20},{16,8},{20,12},{24,0},{28,4},{1,25},{... | collective-permute-start | bytes 1474568 | tf_op jit(solution)/shard_map/ppermute | solution.py:164
  27.7 24.3 %collective-permute-start.13 = (bf16[2,160,768]{2,1,0:T(8,128)(2,1)}, bf16[2,160,768]{2,1,0:T(8,128)(2,1)}, u32[]{:S(2)}, u32[]{:S(2)}) collective-permute-start(bf16[2,160,768]{2,1,0:T(8,128)(2,1)} %get-tuple-element.116.refs_1_), channel_id=1, source_target_pairs={{0,4},{4,0},{8,12},{12,8},{16,20},{20,16},{24,28},{28,24},{1,5},{5... | collective-permute-start | bytes 1474568 | tf_op jit(solution)/shard_map/ppermute | solution.py:164
  31.5 33.7 %all-to-all-start = ((bf16[8,96,768]{2,1,0:T(8,128)(2,1)}), bf16[8,96,768]{2,1,0:T(8,128)(2,1)S(1)}, u32[]{:S(2)}, u32[]{:S(2)}) async-start(bf16[8,96,768]{2,1,0:T(8,128)(2,1)} %place_blocks.4.refs_2_), calls=%async_computation | async-start | bytes 2359296 | tf_op jit(solution)/shard_map/all_to_all | solution.py:180
  48.5 21.1 %collective-permute-start.10 = (bf16[2,256,768]{2,1,0:T(8,128)(2,1)}, bf16[2,256,768]{2,1,0:T(8,128)(2,1)S(1)}, u32[]{:S(2)}, u32[]{:S(2)}) collective-permute-start(bf16[2,256,768]{2,1,0:T(8,128)(2,1)} %get-tuple-element.110), channel_id=1, source_target_pairs={{0,8},{4,12},{8,0},{12,4},{16,24},{20,28},{24,16},{28,20},{1,9},{5... | collective-permute-start | bytes 2359304 | tf_op jit(solution)/shard_map/ppermute | solution.py:164
  49.5 36.7 %collective-permute-start.11 = (bf16[2,256,768]{2,1,0:T(8,128)(2,1)}, bf16[2,256,768]{2,1,0:T(8,128)(2,1)S(1)}, u32[]{:S(2)}, u32[]{:S(2)}) collective-permute-start(bf16[2,256,768]{2,1,0:T(8,128)(2,1)} %get-tuple-element.111), channel_id=1, source_target_pairs={{0,16},{4,20},{8,24},{12,28},{16,0},{20,4},{24,8},{28,12},{1,17},{... | collective-permute-start | bytes 2359304 | tf_op jit(solution)/shard_map/ppermute | solution.py:164
  51.0 35.2 %collective-permute-start.12 = (bf16[2,256,768]{2,1,0:T(8,128)(2,1)}, bf16[2,256,768]{2,1,0:T(8,128)(2,1)S(1)}, u32[]{:S(2)}, u32[]{:S(2)}) collective-permute-start(bf16[2,256,768]{2,1,0:T(8,128)(2,1)} %get-tuple-element.112), channel_id=1, source_target_pairs={{0,24},{4,28},{8,16},{12,20},{16,8},{20,12},{24,0},{28,4},{1,25},{... | collective-permute-start | bytes 2359304 | tf_op jit(solution)/shard_map/ppermute | solution.py:164
  57.3 33.6 %collective-permute-start.20 = (bf16[2,256,768]{2,1,0:T(8,128)(2,1)}, bf16[2,256,768]{2,1,0:T(8,128)(2,1)}, u32[]{:S(2)}, u32[]{:S(2)}) collective-permute-start(bf16[2,256,768]{2,1,0:T(8,128)(2,1)} %get-tuple-element.127.refs_1_), channel_id=1, source_target_pairs={{0,4},{4,0},{8,12},{12,8},{16,20},{20,16},{24,28},{28,24},{1,5},{5... | collective-permute-start | bytes 2359304 | tf_op jit(solution)/shard_map/ppermute | solution.py:164
  65.2 49.4 %all-to-all-start.1 = ((bf16[8,160,768]{2,1,0:T(8,128)(2,1)}), bf16[8,160,768]{2,1,0:T(8,128)(2,1)}, u32[]{:S(2)}, u32[]{:S(2)}) async-start(bf16[8,160,768]{2,1,0:T(8,128)(2,1)} %place_blocks.5.refs_7_), calls=%async_computation.1 | async-start | bytes 3932160 | tf_op jit(solution)/shard_map/all_to_all | solution.py:180
  87.3 35.8 %collective-permute-start.17 = (bf16[2,256,1024]{2,1,0:T(8,128)(2,1)}, bf16[2,256,1024]{2,1,0:T(8,128)(2,1)S(1)}, u32[]{:S(2)}, u32[]{:S(2)}) collective-permute-start(bf16[2,256,1024]{2,1,0:T(8,128)(2,1)} %get-tuple-element.121), channel_id=1, source_target_pairs={{0,8},{4,12},{8,0},{12,4},{16,24},{20,28},{24,16},{28,20},{1,9},{5... | collective-permute-start | bytes 3145736 | tf_op jit(solution)/shard_map/ppermute | solution.py:164
  88.3 46.7 %collective-permute-start.18 = (bf16[2,256,1024]{2,1,0:T(8,128)(2,1)}, bf16[2,256,1024]{2,1,0:T(8,128)(2,1)S(1)}, u32[]{:S(2)}, u32[]{:S(2)}) collective-permute-start(bf16[2,256,1024]{2,1,0:T(8,128)(2,1)} %get-tuple-element.122), channel_id=1, source_target_pairs={{0,16},{4,20},{8,24},{12,28},{16,0},{20,4},{24,8},{28,12},{1,17},{... | collective-permute-start | bytes 3145736 | tf_op jit(solution)/shard_map/ppermute | solution.py:164
  89.4 47.2 %collective-permute-start.19 = (bf16[2,256,1024]{2,1,0:T(8,128)(2,1)}, bf16[2,256,1024]{2,1,0:T(8,128)(2,1)S(1)}, u32[]{:S(2)}, u32[]{:S(2)}) collective-permute-start(bf16[2,256,1024]{2,1,0:T(8,128)(2,1)} %get-tuple-element.123), channel_id=1, source_target_pairs={{0,24},{4,28},{8,16},{12,20},{16,8},{20,12},{24,0},{28,4},{1,25},{... | collective-permute-start | bytes 3145736 | tf_op jit(solution)/shard_map/ppermute | solution.py:164
  114.7 74.9 %all-to-all-start.2 = ((bf16[8,256,768]{2,1,0:T(8,128)(2,1)}), bf16[8,256,768]{2,1,0:T(8,128)(2,1)}, u32[]{:S(2)}, u32[]{:S(2)}) async-start(bf16[8,256,768]{2,1,0:T(8,128)(2,1)} %place_blocks.6.refs_8_), calls=%async_computation.2 | async-start | bytes 6291456 | tf_op jit(solution)/shard_map/all_to_all | solution.py:180
  137.5 20.5 %collective-permute-start.24 = (bf16[2,256,768]{2,1,0:T(8,128)(2,1)}, bf16[2,256,768]{2,1,0:T(8,128)(2,1)S(1)}, u32[]{:S(2)}, u32[]{:S(2)}) collective-permute-start(bf16[2,256,768]{2,1,0:T(8,128)(2,1)} %get-tuple-element.131), channel_id=1, source_target_pairs={{0,8},{4,12},{8,0},{12,4},{16,24},{20,28},{24,16},{28,20},{1,9},{5... | collective-permute-start | bytes 2359304 | tf_op jit(solution)/shard_map/ppermute | solution.py:164
  138.7 36.8 %collective-permute-start.25 = (bf16[2,256,768]{2,1,0:T(8,128)(2,1)}, bf16[2,256,768]{2,1,0:T(8,128)(2,1)}, u32[]{:S(2)}, u32[]{:S(2)}) collective-permute-start(bf16[2,256,768]{2,1,0:T(8,128)(2,1)} %get-tuple-element.132), channel_id=1, source_target_pairs={{0,16},{4,20},{8,24},{12,28},{16,0},{20,4},{24,8},{28,12},{1,17},{... | collective-permute-start | bytes 2359304 | tf_op jit(solution)/shard_map/ppermute | solution.py:164
  140.2 35.3 %collective-permute-start.26 = (bf16[2,256,768]{2,1,0:T(8,128)(2,1)}, bf16[2,256,768]{2,1,0:T(8,128)(2,1)}, u32[]{:S(2)}, u32[]{:S(2)}) collective-permute-start(bf16[2,256,768]{2,1,0:T(8,128)(2,1)} %get-tuple-element.133), channel_id=1, source_target_pairs={{0,24},{4,28},{8,16},{12,20},{16,8},{20,12},{24,0},{28,4},{1,25},{... | collective-permute-start | bytes 2359304 | tf_op jit(solution)/shard_map/ppermute | solution.py:164
  141.0 36.2 %collective-permute-start.31 = (bf16[2,256,768]{2,1,0:T(8,128)(2,1)}, bf16[2,256,768]{2,1,0:T(8,128)(2,1)}, u32[]{:S(2)}, u32[]{:S(2)}) collective-permute-start(bf16[2,256,768]{2,1,0:T(8,128)(2,1)} %get-tuple-element.147.refs_1_), channel_id=1, source_target_pairs={{0,4},{4,0},{8,12},{12,8},{16,20},{20,16},{24,28},{28,24},{1,5},{5... | collective-permute-start | bytes 2359304 | tf_op jit(solution)/shard_map/ppermute | solution.py:164
  176.1 20.7 %collective-permute-start.28 = (bf16[256,1536]{1,0:T(8,128)(2,1)}, bf16[256,1536]{1,0:T(8,128)(2,1)}, u32[]{:S(2)}, u32[]{:S(2)}) collective-permute-start(bf16[256,1536]{1,0:T(8,128)(2,1)} %get-tuple-element.144), channel_id=1, source_target_pairs={{0,8},{4,12},{8,0},{12,4},{16,24},{20,28},{24,16},{28,20},{1,9},{5... | collective-permute-start | bytes 2359304 | tf_op jit(solution)/shard_map/ppermute | solution.py:164
  177.3 35.2 %collective-permute-start.29 = (bf16[256,1536]{1,0:T(8,128)(2,1)}, bf16[256,1536]{1,0:T(8,128)(2,1)}, u32[]{:S(2)}, u32[]{:S(2)}) collective-permute-start(bf16[256,1536]{1,0:T(8,128)(2,1)} %get-tuple-element.145), channel_id=1, source_target_pairs={{0,16},{4,20},{8,24},{12,28},{16,0},{20,4},{24,8},{28,12},{1,17},{... | collective-permute-start | bytes 2359304 | tf_op jit(solution)/shard_map/ppermute | solution.py:164
  178.2 35.9 %collective-permute-start.30 = (bf16[256,1536]{1,0:T(8,128)(2,1)}, bf16[256,1536]{1,0:T(8,128)(2,1)}, u32[]{:S(2)}, u32[]{:S(2)}) collective-permute-start(bf16[256,1536]{1,0:T(8,128)(2,1)} %get-tuple-element.146), channel_id=1, source_target_pairs={{0,24},{4,28},{8,16},{12,20},{16,8},{20,12},{24,0},{28,4},{1,25},{... | collective-permute-start | bytes 2359304 | tf_op jit(solution)/shard_map/ppermute | solution.py:164
  189.5 80.8 %all-to-all-start.3 = ((bf16[8,256,768]{2,1,0:T(8,128)(2,1)}), bf16[8,256,768]{2,1,0:T(8,128)(2,1)S(1)}, u32[]{:S(2)}, u32[]{:S(2)}) async-start(bf16[8,256,768]{2,1,0:T(8,128)(2,1)} %place_blocks.7.refs_3_), calls=%async_computation.3 | async-start | bytes 6291456 | tf_op jit(solution)/shard_map/all_to_all | solution.py:180
  222.7 19.4 %collective-permute-start.38 = (bf16[256,1536]{1,0:T(8,128)(2,1)}, bf16[256,1536]{1,0:T(8,128)(2,1)}, u32[]{:S(2)}, u32[]{:S(2)}) collective-permute-start(bf16[256,1536]{1,0:T(8,128)(2,1)} %get-tuple-element.154.refs_1_.refs_8_), channel_id=1, source_target_pairs={{0,16},{4,20},{8,24},{12,28},{16,0},{20,4},{24,8},{28,12},{1,17},{... | collective-permute-start | bytes 2359304 | tf_op jit(solution)/shard_map/ppermute | solution.py:164
  242.3 19.1 %collective-permute-start.47 = (bf16[256,1536]{1,0:T(8,128)(2,1)}, bf16[256,1536]{1,0:T(8,128)(2,1)}, u32[]{:S(2)}, u32[]{:S(2)}) collective-permute-start(bf16[256,1536]{1,0:T(8,128)(2,1)} %gate.19), channel_id=1, source_target_pairs={{0,24},{4,28},{8,16},{12,20},{16,8},{20,12},{24,0},{28,4},{1,25},{... | collective-permute-start | bytes 2359304 | tf_op jit(solution)/shard_map/ppermute | solution.py:164
  243.8 19.2 %collective-permute-start.40 = (bf16[2,256,1024]{2,1,0:T(8,128)(2,1)}, bf16[2,256,1024]{2,1,0:T(8,128)(2,1)}, u32[]{:S(2)}, u32[]{:S(2)}) collective-permute-start(bf16[2,256,1024]{2,1,0:T(8,128)(2,1)} %get-tuple-element.134.refs_0_), channel_id=1, source_target_pairs={{0,4},{4,0},{8,12},{12,8},{16,20},{20,16},{24,28},{28,24},{1,5},{5... | collective-permute-start | bytes 3145736 | tf_op jit(solution)/shard_map/ppermute | solution.py:164
  243.8 19.2 %collective-permute-start.41 = (bf16[2,256,1024]{2,1,0:T(8,128)(2,1)}, bf16[2,256,1024]{2,1,0:T(8,128)(2,1)}, u32[]{:S(2)}, u32[]{:S(2)}) collective-permute-start(bf16[2,256,1024]{2,1,0:T(8,128)(2,1)} %get-tuple-element.135.refs_1_.refs_2_), channel_id=1, source_target_pairs={{0,4},{4,0},{8,12},{12,8},{16,20},{20,16},{24,28},{28,24},{1,5},{5... | collective-permute-start | bytes 3145736 | tf_op jit(solution)/shard_map/ppermute | solution.py:164
  244.3 19.2 %collective-permute-start.42 = (bf16[2,256,1024]{2,1,0:T(8,128)(2,1)}, bf16[2,256,1024]{2,1,0:T(8,128)(2,1)}, u32[]{:S(2)}, u32[]{:S(2)}) collective-permute-start(bf16[2,256,1024]{2,1,0:T(8,128)(2,1)} %get-tuple-element.136.refs_2_.refs_4_), channel_id=1, source_target_pairs={{0,4},{4,0},{8,12},{12,8},{16,20},{20,16},{24,28},{28,24},{1,5},{5... | collective-permute-start | bytes 3145736 | tf_op jit(solution)/shard_map/ppermute | solution.py:164
  244.3 19.3 %collective-permute-start.43 = (bf16[2,256,1024]{2,1,0:T(8,128)(2,1)}, bf16[2,256,1024]{2,1,0:T(8,128)(2,1)}, u32[]{:S(2)}, u32[]{:S(2)}) collective-permute-start(bf16[2,256,1024]{2,1,0:T(8,128)(2,1)} %get-tuple-element.137.refs_3_.refs_6_), channel_id=1, source_target_pairs={{0,4},{4,0},{8,12},{12,8},{16,20},{20,16},{24,28},{28,24},{1,5},{5... | collective-permute-start | bytes 3145736 | tf_op jit(solution)/shard_map/ppermute | solution.py:164
  261.5 26.4 %collective-permute-start.39 = (bf16[2,4,256,256]{3,2,1,0:T(8,128)(2,1)}, bf16[2,4,256,256]{3,2,1,0:T(8,128)(2,1)}, u32[]{:S(2)}, u32[]{:S(2)}) collective-permute-start(bf16[2,4,256,256]{3,2,1,0:T(8,128)(2,1)} %get-tuple-element.162), channel_id=1, source_target_pairs={{0,1},{1,0},{2,3},{3,2},{4,5},{5,4},{6,7},{7,6},{8,9},{9,8},{10,11... | collective-permute-start | bytes 3145736 | tf_op jit(solution)/shard_map/ppermute | solution.py:168
  269.8 37.3 %collective-permute-start.52 = (bf16[2,2,256,256]{3,2,1,0:T(8,128)(2,1)}, bf16[2,2,256,256]{3,2,1,0:T(8,128)(2,1)}, u32[]{:S(2)}, u32[]{:S(2)}) collective-permute-start(bf16[2,2,256,256]{3,2,1,0:T(8,128)(2,1)} %get-tuple-element.170), channel_id=1, source_target_pairs={{0,1},{1,0},{2,3},{3,2},{4,5},{5,4},{6,7},{7,6},{8,9},{9,8},{10,11... | collective-permute-start | bytes 1572872 | tf_op jit(solution)/shard_map/ppermute | solution.py:168
  290.7 25.2 %collective-permute-start.49 = (bf16[1,4,256,256]{3,2,1,0:T(8,128)(2,1)}, bf16[1,4,256,256]{3,2,1,0:T(8,128)(2,1)S(1)}, u32[]{:S(2)}, u32[]{:S(2)}) collective-permute-start(bf16[1,4,256,256]{3,2,1,0:T(8,128)(2,1)} %get-tuple-element.166), channel_id=1, source_target_pairs={{0,2},{1,3},{2,0},{3,1},{4,6},{5,7},{6,4},{7,5},{8,10},{9,11},{10,... | collective-permute-start | bytes 1572872 | tf_op jit(solution)/shard_map/ppermute | solution.py:168
  293.3 31.8 %collective-permute-start.35 = (bf16[2,2,256,256]{3,2,1,0:T(8,128)(2,1)S(1)}, bf16[2,2,256,256]{3,2,1,0:T(8,128)(2,1)S(1)}, u32[]{:S(2)}, u32[]{:S(2)}) collective-permute-start(bf16[2,2,256,256]{3,2,1,0:T(8,128)(2,1)S(1)} %copy-done.31), channel_id=1, source_target_pairs={{0,1},{1,0},{2,3},{3,2},{4,5},{5,4},{6,7},{7,6},{8,9},{9,8},{10,11... | collective-permute-start | bytes 1572872 | tf_op jit(solution)/shard_map/ppermute | solution.py:168
  (59 other events, 330.0 us)
